TPU v7x, 32 devices: a whole 2x2x4 slice. The times are simulated.
32 devices in a mesh: dp: 2 (over core), ctx: 8 (over z, y), tp: 2 (over x).
Axes of the slice: x: 2, y: 2, z: 4, core: 2. Of those that a mesh axis runs over, the one named last changes fastest.
Arguments:
- teacher_part: bfloat16 [2, 2, 2048, 8192], P('dp', 'tp', 'ctx'), may hold values from -8 to 8
- student_in: bfloat16 [2, 2048, 4096], P('dp', 'ctx'), may hold values from -24 to 24
- out_proj: bfloat16 [4096, 4096], P('ctx', 'tp'), may hold values from -0.09375 to 0.09375
- segment_ids: int32 [2, 2048], P('dp'), may hold values from 0 to 3, never falling along the last dimension, each value on 1 to 1024 neighbouring positions
- valid_count: int32 [2], P('dp'), may hold values from 256 to 2048, as said below
Outputs:
- doc_loss: float32 [2], P('dp')
- wo_grad: float32 [4096, 4096], P('ctx', 'tp')
- state_grad: float32 [2, 2048, 4096], P('dp', 'ctx', 'tp')
Inputs may be any that keep to these rules, and one draw needn't show every extreme that they name: `valid_count`: one document in every draw is valid at all 2048 positions. `segment_ids`: segment numbers never fall along a document.
All inputs are finite; a program needn't handle non-finite values.
Results may differ from a plain program's by a relative error of at most 0.019.
The roundings to bfloat16 on the way count: a program that leaves them out, or rounds other values in their place, can miss the bound.
Values may be sent and summed in bfloat16 or wider, within the bound.
No kernel may reach another device: no remote copies, remote signals or barrier semaphores. Data moves between devices by JAX's collectives and lax.ppermute only.
A program may use at most 64 MiB of HBM per device.

v0:
```python
import math

import jax
import jax.numpy as jnp
from jax import lax
from jax.sharding import PartitionSpec as P

DS = 4096
HEADS = 32


masked_score = -1e30


def shifted_2(value, axis, steps):
    count = lax.axis_size(axis)
    leading, last = (max(0, -steps), min(count, count - steps))
    return lax.ppermute(value, axis, [(source, source + steps) for source in range(leading, last)])


def log_probs(scores, allowed):
    scores = jnp.where(allowed[None, :, :], scores, masked_score)
    top = jnp.max(scores, axis=-1, keepdims=True)
    shifted = scores - top
    return shifted - jnp.log(jnp.sum(jnp.exp(shifted), axis=-1, keepdims=True))


def window_terms(
    teacher_query, teacher_keys, student_query, student_keys, allowed, live, head_count
):
    length = teacher_query.shape[0]
    teacher_qh = teacher_query.reshape(length, head_count, -1)
    teacher_kh = teacher_keys.reshape(2 * length, head_count, -1)
    student_qh = student_query.reshape(length, head_count, -1)
    student_kh = student_keys.reshape(2 * length, head_count, -1)
    teacher_scale = 1.0 / math.sqrt(teacher_qh.shape[-1])
    student_scale = 1.0 / math.sqrt(student_qh.shape[-1])
    teacher_scores = (
        jnp.einsum("qhd,khd->hqk", teacher_qh, teacher_kh, preferred_element_type=jnp.float32)
        * teacher_scale
    )
    student_scores = (
        jnp.einsum("qhd,khd->hqk", student_qh, student_kh, preferred_element_type=jnp.float32)
        * student_scale
    )
    teacher_logp = log_probs(teacher_scores, allowed)
    student_logp = log_probs(student_scores, allowed)
    teacher_prob = jnp.exp(teacher_logp)
    student_prob = jnp.exp(student_logp)
    divergence = jnp.sum(teacher_prob * (teacher_logp - student_logp), axis=-1)
    loss_part = jnp.sum(divergence * live[None, :]) / HEADS
    grad_scale = live[None, :, None] * (student_scale / HEADS)
    score_grad = ((student_prob - teacher_prob) * grad_scale).astype(jnp.bfloat16)
    query_grad = jnp.einsum(
        "hqk,khd->qhd", score_grad, student_kh, preferred_element_type=jnp.float32
    ).reshape(length, -1)
    key_grad = jnp.einsum(
        "hqk,qhd->khd", score_grad, student_qh, preferred_element_type=jnp.float32
    ).reshape(2 * length, -1)
    return (loss_part, query_grad, key_grad)


def per_device(teacher_part, student_in, out_proj, segment_ids, valid_count):
    window_len = student_in.shape[1]
    head_count = HEADS // lax.axis_size("tp")
    unscale = HEADS * math.sqrt(DS // HEADS)
    partial_sum = teacher_part[0, 0].astype(jnp.float32)
    teacher_own = lax.psum_scatter(
        partial_sum.astype(jnp.bfloat16), "tp", scatter_dimension=1, tiled=True
    )
    tokens = student_in[0]
    columns = tokens
    student_own = jnp.dot(
        columns,
        lax.all_gather(out_proj, "ctx", axis=0, tiled=True),
        preferred_element_type=jnp.float32,
    ).astype(jnp.bfloat16)
    teacher_prev, student_prev = shifted_2((teacher_own, student_own), "ctx", 1)
    teacher_keys = jnp.concatenate([teacher_prev, teacher_own], 0)
    student_keys = jnp.concatenate([student_prev, student_own], 0)
    window = lax.axis_index("ctx")
    start = window * window_len
    segments = segment_ids[0]
    segment_padded = jnp.concatenate([jnp.full((window_len,), -1, jnp.int32), segments], 0)
    query_segment = lax.dynamic_slice_in_dim(segments, start, window_len, 0)
    key_segment = lax.dynamic_slice_in_dim(segment_padded, start, 2 * window_len, 0)
    valid_limit = valid_count[0]
    query_position = start + jnp.arange(window_len, dtype=jnp.int32)
    key_position = start - window_len + jnp.arange(2 * window_len, dtype=jnp.int32)
    allowed = (key_segment[None, :] == query_segment[:, None]) & (
        key_position[None, :] < valid_limit
    )
    live = jnp.where(query_position < valid_limit, 1.0, 0.0).astype(jnp.float32)
    loss_part, query_grad, key_grad = window_terms(
        teacher_own, teacher_keys, student_own, student_keys, allowed, live, head_count
    )
    from_next = shifted_2(key_grad[:window_len].astype(jnp.bfloat16), "ctx", -1).astype(jnp.float32)
    hidden_grad = (query_grad + key_grad[window_len:] + from_next).astype(jnp.bfloat16)
    state_grad = (hidden_grad.astype(jnp.float32) * unscale)[None]
    columns = tokens
    grad_piece = lax.psum_scatter(
        jnp.einsum("tr,tc->rc", columns, hidden_grad, preferred_element_type=jnp.float32).astype(
            jnp.bfloat16
        ),
        "ctx",
        scatter_dimension=0,
        tiled=True,
    )
    wo_grad = lax.psum(grad_piece, "dp").astype(jnp.float32)
    doc_loss = lax.psum(loss_part, ("ctx", "tp"))
    return (doc_loss.reshape(1), wo_grad, state_grad)


def solution(mesh):
    return jax.shard_map(
        per_device,
        mesh=mesh,
        in_specs=(
            P("dp", "tp", "ctx", None),
            P("dp", "ctx", None),
            P("ctx", "tp"),
            P("dp", None),
            P("dp"),
        ),
        out_specs=(P("dp"), P("ctx", "tp"), P("dp", "ctx", "tp")),
        check_vma=False,
    )
```

profile of v0, /device:TPU:1, one launch (start us, length us, event | category | flops | bytes accessed | tf_op | source)
XLA Modules:
  0.0 714.8 jit_solution(4276560208564486889)
XLA Ops:
  8.1 6.5 copy.32
  14.6 0.5 all-gather.2.cloned.1.call-update
  15.2 55.9 %reduce-scatter.3.cloned.1.call-done = bf16[256,4096]{0,1:T(8,128)(2,1)} async-done(((bf16[256,8192]{0,1:T(8,128)(2,1)}), bf16[256,4096]{0,1:T(8,128)(2,1)}) %reduce-scatter.3.cloned.1.call-update) | async-done | bytes 2097168 | tf_op jit(solution)/shard_map/reduce_scatter | solution.py:68
  71.2 4.4 collective-permute-start
  76.4 0.2 compare_and_fusion
  76.6 42.3 %collective-permute-done = bf16[256,4096]{0,1:T(8,128)(2,1)} collective-permute-done((bf16[256,4096]{0,1:T(8,128)(2,1)}, bf16[256,4096]{0,1:T(8,128)(2,1)}, u32[]{:S(2)}, u32[]{:S(2)}) %collective-permute-start) | collective-permute-done | bytes 2097184 | tf_op jit(solution)/shard_map/ppermute | solution.py:18
  118.9 4.5 pad_maximum_fusion
  123.4 160.3 %all-gather.2.cloned.1.call-done = bf16[4096,2048]{1,0:T(8,128)(2,1)} async-done(((bf16[512,2048]{1,0:T(8,128)(2,1)}), bf16[4096,2048]{1,0:T(8,128)(2,1)}) %all-gather.2.cloned.1.call-update) | async-done | bytes 16777232 | tf_op jit(solution)/shard_map/all_gather | solution.py:75
  283.7 9.2 %convolution_convert_fusion = bf16[256,2048]{1,0:T(8,128)(2,1)} fusion(bf16[4096,2048]{1,0:T(8,128)(2,1)} %all-gather.2.cloned.1.call-done, bf16[1,256,4096]{2,1,0:T(8,128)(2,1)S(1)} %copy-done), kind=kOutput, calls=%fused_computation.26 | convolution fusion | flops 4295491584 | bytes 19922944 | tf_op jit(solution)/shard_map/dot_general | solution.py:73
  293.0 2.3 collective-permute-start.1
  295.2 8.7 %fusion.8 = f32[16,256,512]{1,2,0:T(8,128)} fusion(pred[256,512]{0,1:T(8,128)(4,1)S(1)} %compare_and_fusion, bf16[512,16,256]{0,2,1:T(8,128)(2,1)} %bitcast.54, bf16[256,16,256]{0,2,1:T(8,128)(2,1)} %bitcast.56), kind=kOutput, calls=%fused_computation.17 | convolution fusion | flops 1080037888 | bytes 14811136 | tf_op jit(solution)/shard_map/sub | solution.py:24
  303.9 10.5 %log_subtract_fusion.1 = f32[16,256,512]{1,2,0:T(8,128)} fusion(f32[16,256,512]{1,2,0:T(8,128)} %fusion.8), kind=kOutput, calls=%fused_computation.6 | output fusion | flops 2101759 | bytes 16777216 | tf_op jit(solution)/shard_map/reduce_sum | solution.py:25
  314.4 1.5 copy.50
  315.9 0.5 collective-permute-done.1
  316.4 3.1 pad_maximum_fusion.1
  319.5 3.9 copy.51
  323.4 7.2 %fusion.6 = f32[16,256,512]{1,2,0:T(8,128)} fusion(pred[256,512]{0,1:T(8,128)(4,1)S(1)} %compare_and_fusion, bf16[256,16,128]{0,2,1:T(8,128)(2,1)S(1)} %bitcast.52, bf16[512,16,128]{0,2,1:T(8,128)(2,1)} %bitcast.49), kind=kOutput, calls=%fused_computation.15 | convolution fusion | flops 543166976 | bytes 11665408 | tf_op jit(solution)/shard_map/sub | solution.py:24
  330.7 10.8 %multiply_convert_fusion = (bf16[16,256,512]{1,2,0:T(8,128)(2,1)S(1)}, f32[16,256]{1,0:T(8,128)S(1)}) fusion(f32[16,256,512]{1,2,0:T(8,128)} %log_subtract_fusion.1, f32[256]{0:T(256)S(1)} %get-tuple-element.15, f32[16,256,512]{1,2,0:T(8,128)} %fusion.6), kind=kOutput, calls=%fused_computation.8 | output fusion | flops 14680575 | bytes 20988928 | tf_op jit(solution)/shard_map/reduce_sum | solution.py:25
  341.4 1.5 convolution_bitcast_fusion
  342.9 0.4 copy-done.1
  343.5 1.9 copy-done.2
  345.4 1.4 copy.42
  346.8 1.5 collective-permute-start.2
  348.3 5.5 slice_add_fusion
  353.9 2.9 copy.43
  356.7 16.3 %collective-permute-done.2 = bf16[256,2048]{1,0:T(8,128)(2,1)S(1)} collective-permute-done((bf16[256,2048]{1,0:T(8,128)(2,1)}, bf16[256,2048]{1,0:T(8,128)(2,1)S(1)}, u32[]{:S(2)}, u32[]{:S(2)}) %collective-permute-start.2) | collective-permute-done | bytes 1048608 | tf_op jit(solution)/shard_map/ppermute | solution.py:18
  373.0 9.7 %convert_bitcast_fusion = bf16[4096,2048]{0,1:T(8,128)(2,1)} fusion(bf16[1,256,4096]{2,1,0:T(8,128)(2,1)S(1)} %copy-done, f32[256,2048]{1,0:T(8,128)} %copy.43, bf16[256,2048]{1,0:T(8,128)(2,1)S(1)} %collective-permute-done.2), kind=kOutput, calls=%fused_computation.4 | convolution fusion | flops 4304928768 | bytes 22020096 | tf_op jit(solution)/shard_map/tr,tc->rc/dot_general | solution.py:102
  382.8 281.7 %reduce-scatter.5.cloned.1.call-done = bf16[512,2048]{0,1:T(8,128)(2,1)} async-done(((bf16[4096,2048]{0,1:T(8,128)(2,1)}), bf16[512,2048]{0,1:T(8,128)(2,1)}) %reduce-scatter.5.cloned.1.call-update) | async-done | bytes 2097168 | tf_op jit(solution)/shard_map/reduce_scatter | solution.py:101
  664.6 0.6 multiply_reduce_fusion.1
  665.8 34.2 %psum.14 = f32[1]{0:T(128)} all-reduce(f32[1]{0:T(128)} %bitcast.8), channel_id=1, replica_groups=mesh['dp'=2,'ctx'=8,'tp'=2] {'ctx','tp'}, use_global_device_ids=true, to_apply=%region_7.8 | all-reduce | flops 1 | bytes 8 | tf_op jit(solution)/shard_map/psum | solution.py:110
  700.0 3.3 multiply_bitcast_fusion
  703.3 4.1 copy.44
  (19 shorter events, 0.5 us)
Async XLA Ops:
  8.0 275.7 %copy-start = (bf16[1,256,4096]{2,1,0:T(8,128)(2,1)S(1)}, bf16[1,256,4096]{2,1,0:T(8,128)(2,1)}, u32[]{:S(2)}) copy-start(bf16[1,256,4096]{2,1,0:T(8,128)(2,1)} %param.6) | copy-start | bytes 6291460
  8.0 63.2 %reduce-scatter.3.cloned.1.call-start = ((), (), s32[]{:S(2)}) async-start(), calls=%async_computation.2 | async-start | bytes 6291456 | tf_op jit(solution)/shard_map/reduce_scatter | solution.py:68
  14.6 61.7 %copy-start.3 = (s32[1,2048]{1,0:T(1,128)S(1)}, s32[1,2048]{1,0:T(1,128)}, u32[]{:S(2)}) copy-start(s32[1,2048]{1,0:T(1,128)} %param.8) | copy-start | bytes 24580
  14.6 269.1 %all-gather.2.cloned.1.call-start = ((), (), s32[]{:S(2)}) async-start(), calls=%async_computation.3 | async-start | bytes 18874368 | tf_op jit(solution)/shard_map/all_gather | solution.py:75
  15.2 649.4 %reduce-scatter.5.cloned.1.call-start = ((), (), s32[]{:S(2)}) async-start(), calls=%async_computation.4 | async-start | bytes 18874368 | tf_op jit(solution)/shard_map/reduce_scatter | solution.py:101
  71.2 47.7 %collective-permute-start = (bf16[256,4096]{0,1:T(8,128)(2,1)}, bf16[256,4096]{0,1:T(8,128)(2,1)}, u32[]{:S(2)}, u32[]{:S(2)}) collective-permute-start(bf16[256,4096]{0,1:T(8,128)(2,1)} %reduce-scatter.3.cloned.1.call-done), channel_id=1, source_target_pairs={{0,2},{2,4},{4,6},{6,8},{8,10},{10,12},{12,14},{1,3},{3,5},{5,7},{... | collective-permute-start | bytes 6291464 | tf_op jit(solution)/shard_map/ppermute | solution.py:18
  293.0 23.4 %collective-permute-start.1 = (bf16[256,2048]{1,0:T(8,128)(2,1)}, bf16[256,2048]{1,0:T(8,128)(2,1)}, u32[]{:S(2)}, u32[]{:S(2)}) collective-permute-start(bf16[256,2048]{1,0:T(8,128)(2,1)} %convolution_convert_fusion), channel_id=1, source_target_pairs={{0,2},{2,4},{4,6},{6,8},{8,10},{10,12},{12,14},{1,3},{3,5},{5,7},{... | collective-permute-start | bytes 3145736 | tf_op jit(solution)/shard_map/ppermute | solution.py:18
  341.4 1.9 copy-start.1
  343.4 2.0 copy-start.2
  346.8 26.2 %collective-permute-start.2 = (bf16[256,2048]{1,0:T(8,128)(2,1)}, bf16[256,2048]{1,0:T(8,128)(2,1)S(1)}, u32[]{:S(2)}, u32[]{:S(2)}) collective-permute-start(bf16[256,2048]{1,0:T(8,128)(2,1)} %copy.42), channel_id=1, source_target_pairs={{2,0},{4,2},{6,4},{8,6},{10,8},{12,10},{14,12},{3,1},{5,3},{7,5},{... | collective-permute-start | bytes 3145736 | tf_op jit(solution)/shard_map/ppermute | solution.py:18
  382.8 320.5 %all-reduce.3.cloned.1.call-start = ((), (), s32[]{:S(2)}) async-start(), calls=%async_computation.5 | async-start | bytes 4194304 | tf_op jit(solution)/shard_map/psum | solution.py:109
Sparse Core Ops, SparseCore 0:
  14.7 56.4 reduce-scatter.2
  664.7 20.9 all-reduce.2
Sparse Core Ops, SparseCore 1:
  17.4 266.3 all-gather.1
  382.9 281.6 reduce-scatter.4
where the time goes:
time: 723 us; the launch traced here: 715 us
  waiting for transfers between devices  558 us (77%)
  matrix products  41.9 us (6%)
  blocking collectives  34.2 us (5%)
  other arithmetic  33 us (5%)
  local copies, waits for them, and re-layouts  22.9 us (3%)
  between operations  16.9 us (2%)
  starting transfers between devices  8.33 us (1%)
    reduce_scatter x1, waiting for transfers between devices, per_device(): lax.psum_scatter(jnp.einsum('tr,tc->rc', columns, hidden_grad, preferred_...  282 us
    all_gather x1, waiting for transfers between devices, per_device(): lax.all_gather(out_proj, 'ctx', axis=0, tiled=True)  160 us
    ppermute x3, waiting for transfers between devices, shifted_2(): lax.ppermute(value, axis, [(source, source + steps) for source in range(l...  59.1 us
    reduce_scatter x1, waiting for transfers between devices, per_device(): lax.psum_scatter(partial_sum.astype(jnp.bfloat16), 'tp', scatter_dimensio...  55.9 us
    psum x1, blocking collectives, per_device(): doc_loss = lax.psum(loss_part, ('ctx', 'tp'))  34.2 us
    reduce_sum x2, other arithmetic, log_probs(): return shifted - jnp.log(jnp.sum(jnp.exp(shifted), axis=-1, keepdims=True))  21.2 us
    sub x2, matrix products, log_probs(): shifted = scores - top  15.9 us
  transfers between devices with their start and end apart: 7, of which 6 were waited for; matrix products, arithmetic and copies ran while one was open for 5% of the time, Pallas kernels for 0%

commit v1 on v0

v1 whole, which is shorter than its diff:
```python
import functools
import math

import jax
import jax.numpy as jnp
from jax import lax
from jax.experimental import pallas as pl
from jax.experimental.layout import Layout, with_layout_constraint
from jax.experimental.pallas import tpu as pltpu
from jax.sharding import PartitionSpec as P

DS = 4096
HEADS = 32
CHUNKS = 2
HEADS_A_STEP = 2
MASKED = -1e30


def after(value, *earlier):
    return lax.optimization_barrier((value, *earlier))[0]


def row_major(value):
    return with_layout_constraint(value, Layout(tuple(range(value.ndim))))


def rotate(value, axis, steps):
    count = lax.axis_size(axis)
    return lax.ppermute(value, axis, [(i, (i + steps) % count) for i in range(count)])


def swap(value, axis, distance):
    count = lax.axis_size(axis)
    return lax.ppermute(value, axis, [(i, i ^ distance) for i in range(count)])


def shift(value, axis, steps):
    count = lax.axis_size(axis)
    pairs = [(i, i + steps) for i in range(count) if 0 <= i + steps < count]
    return lax.ppermute(value, axis, pairs)


def ordered(mine, other, place):
    first = lax.select(place == 0, mine, other)
    second = lax.select(place == 0, other, mine)
    return first, second


def send_line(value, axis, upward=(), downward=()):
    pairs = [(2 * i + j, 2 * i + 2 + j) for i in upward for j in range(2)]
    pairs += [(2 * i + j, 2 * i - 2 + j) for i in downward for j in range(2)]
    return lax.ppermute(value, axis, pairs)


def gather_line(block, axis, gates):
    groups, group = lax.axis_size(axis) // 2, lax.axis_index(axis) >> 1
    out, up, down, either = [(group, block)], block, block, None
    for hop in range(1, groups):
        upward, downward = range(hop - 1, groups - 1), range(1, groups - hop + 1)
        gate = gates.get(hop, ())
        below, above = jnp.maximum(group - hop, 0), jnp.minimum(group + hop, groups - 1)
        if either is None:
            if gate:
                up, down = after(up, *gate), after(down, *gate)
            up = send_line(up, axis, upward=upward)
            down = send_line(down, axis, downward=downward)
            if 2 * hop < groups:
                out += [(below, up), (above, down)]
                continue
            either = lax.select(group >= hop, up, down)
        else:
            if gate:
                either = after(either, *gate)
            either = send_line(either, axis, upward, downward)
        out.append((lax.select(group >= hop, below, above), either))
    return out


def scatter_line(blocks, axis):
    groups, group = lax.axis_size(axis) // 2, lax.axis_index(axis) >> 1

    def plus(target, came):
        block = lax.dynamic_index_in_dim(blocks, target, 0, keepdims=False)
        return block if came is None else block + came.astype(jnp.float32)

    up = down = None
    for step in range(1, groups):
        upward, downward = range(min(step, groups - 1)), range(max(groups - step, 1), groups)
        rising = plus(jnp.minimum(groups - step + group, groups - 1), up).astype(jnp.bfloat16)
        falling = plus(jnp.maximum(group + step - groups, 0), down).astype(jnp.bfloat16)
        if 2 * step < groups - 1:
            value = lax.select(group < step, rising, falling)
            came = send_line(value, axis, upward, downward)
            none = jnp.zeros_like(came)
            up = lax.select(group <= step, came, none)
            down = lax.select(group >= groups - 1 - step, came, none)
        else:
            up = send_line(rising, axis, upward=upward)
            down = send_line(falling, axis, downward=downward)
    return plus(group, up) + down.astype(jnp.float32), (up, down)


def by_owner(parts, me):
    count = len(parts)
    if count == 2:
        return ordered(*parts, me)
    parts = jnp.stack(parts)
    return [
        lax.dynamic_index_in_dim(parts, lax.rem(me + count - i, count), 0, keepdims=False)
        for i in range(count)
    ]


def split_kernel(count, rows, tokens, out):
    width = tokens.shape[1] // count // rows
    for piece in range(count):
        for row in range(rows):
            start = (row * count + piece) * width
            out[piece, :, row * width : (row + 1) * width] = tokens[:, start : start + width]


def split(tokens, blocks, count):
    length, width = tokens.shape
    rows = max(1, 128 * blocks * count // width)
    step = width // blocks * rows
    return pl.pallas_call(
        functools.partial(split_kernel, count, rows),
        grid=(blocks // rows,),
        in_specs=[pl.BlockSpec((length, step), lambda i: (0, i))],
        out_specs=pl.BlockSpec((count, length, step // count), lambda i: (0, 0, i)),
        out_shape=jax.ShapeDtypeStruct((count, length, width // count), tokens.dtype),
        compiler_params=pltpu.CompilerParams(vmem_limit_bytes=16 * 1024 * 1024),
        cost_estimate=pl.CostEstimate(
            flops=0, bytes_accessed=4 * length * width, transcendentals=0
        ),
        name="split_tokens",
    )(tokens)


def attention_kernel(teacher_scale, student_scale, grad_scale, heads, *refs):
    teacher, student = refs[0:3], refs[3:6]
    bias, live, loss = refs[6], refs[7], refs[8]
    grad_past, grad_first, grad_second = refs[9:12]
    length = student[0].shape[0]
    dt, ds = teacher[0].shape[1] // heads, student[0].shape[1] // heads
    log2e = math.log2(math.e)

    @pl.when(pl.program_id(0) == 0)
    def _():
        loss[...] = jnp.zeros_like(loss)

    def scores(keys, queries, scale, mask):
        product = lax.dot_general(
            keys, queries, (((1,), (1,)), ((), ())), preferred_element_type=jnp.float32
        )
        return product * (scale * log2e) + mask

    def soft(first, second):
        top = jnp.maximum(
            jnp.max(first, axis=0, keepdims=True), jnp.max(second, axis=0, keepdims=True)
        )
        first, second = first - top, second - top
        e_first, e_second = jnp.exp2(first), jnp.exp2(second)
        total = jnp.sum(e_first, axis=0, keepdims=True) + jnp.sum(e_second, axis=0, keepdims=True)
        return first, second, e_first, e_second, total

    for h in range(heads):
        t_cols, s_cols = slice(h * dt, (h + 1) * dt), slice(h * ds, (h + 1) * ds)
        own = []
        for w in range(2):
            t_past, t_query = teacher[w][:, t_cols], teacher[w + 1][:, t_cols]
            s_past, s_query = student[w][:, s_cols], student[w + 1][:, s_cols]
            bias_past, bias_own = bias[w, :length, :], bias[w, length:, :]
            live_row = live[w]
            t0, t1, te0, te1, t_total = soft(
                scores(t_past, t_query, teacher_scale, bias_past),
                scores(t_query, t_query, teacher_scale, bias_own),
            )
            s0, s1, se0, se1, s_total = soft(
                scores(s_past, s_query, student_scale, bias_past),
                scores(s_query, s_query, student_scale, bias_own),
            )
            gap = jnp.sum(te0 * (t0 - s0), axis=0, keepdims=True) + jnp.sum(
                te1 * (t1 - s1), axis=0, keepdims=True
            )
            t_inverse = 1.0 / t_total
            divergence = gap * t_inverse * math.log(2.0) - (jnp.log(t_total) - jnp.log(s_total))
            loss[...] += divergence * live_row
            t_weight = t_inverse * (live_row * grad_scale)
            s_weight = (live_row * grad_scale) / s_total
            grad0 = (se0 * s_weight - te0 * t_weight).astype(jnp.bfloat16)
            grad1 = (se1 * s_weight - te1 * t_weight).astype(jnp.bfloat16)
            by_past = jnp.dot(grad0, s_query, preferred_element_type=jnp.float32)
            if w == 0:
                grad_past[:, s_cols] = by_past.astype(grad_past.dtype)
            else:
                own[0] = own[0] + by_past
            by_query = jnp.dot(s_past.T, grad0, preferred_element_type=jnp.float32) + jnp.dot(
                s_query.T, grad1, preferred_element_type=jnp.float32
            )
            own.append(
                by_query.T + jnp.dot(grad1, s_query, preferred_element_type=jnp.float32)
            )
        grad_first[:, s_cols] = own[0].astype(grad_first.dtype)
        grad_second[:, s_cols] = own[1]


def attention(teacher, student, bias, live):
    (length, width), ds = student[0].shape, DS // HEADS
    head_count = width // ds
    dt = teacher[0].shape[1] // head_count
    heads = min(HEADS_A_STEP, head_count)
    student_scale = 1.0 / math.sqrt(ds)
    kernel = functools.partial(
        attention_kernel, 1.0 / math.sqrt(dt), student_scale, student_scale / HEADS, heads
    )
    steps = head_count // heads
    inputs = lambda d: pl.BlockSpec((length, heads * d), lambda h: (0, h))
    columns = pl.BlockSpec((length, heads * ds), lambda h: (0, h))
    whole = lambda *shape: pl.BlockSpec(shape, lambda h: (0,) * len(shape))
    flops = 2 * head_count * length * length * (4 * dt + 4 * ds + 8 * ds)
    return pl.pallas_call(
        kernel,
        grid=(steps,),
        in_specs=[inputs(dt)] * 3
        + [inputs(ds)] * 3
        + [whole(2, 2 * length, length), whole(2, 1, length)],
        out_specs=[whole(1, length)] + [columns] * 3,
        out_shape=[
            jax.ShapeDtypeStruct((1, length), jnp.float32),
            jax.ShapeDtypeStruct((length, width), jnp.bfloat16),
            jax.ShapeDtypeStruct((length, width), jnp.bfloat16),
            jax.ShapeDtypeStruct((length, width), jnp.float32),
        ],
        compiler_params=pltpu.CompilerParams(vmem_limit_bytes=24 * 1024 * 1024),
        cost_estimate=pl.CostEstimate(
            flops=flops,
            bytes_accessed=6 * length * (dt + ds) * head_count + 8 * length * width,
            transcendentals=8 * length * length * head_count,
        ),
        name="window_attention",
    )(*teacher, *student, bias, live)


def per_device(teacher_part, student_in, out_proj, segment_ids, valid_count):
    tokens = student_in[0]
    length = tokens.shape[0]
    n_dp, n_tp, n_ctx = lax.axis_size("dp"), lax.axis_size("tp"), lax.axis_size("ctx")
    my_dp, my_tp, window = lax.axis_index("dp"), lax.axis_index("tp"), lax.axis_index("ctx")
    groups, group, place = n_ctx // 2, window >> 1, window & 1
    block_rows, width = out_proj.shape
    piece_rows, my_width = block_rows // n_dp, width // 2
    chunk_width = my_width // CHUNKS
    teacher_width = teacher_part.shape[3] // n_tp
    teacher_chunk = teacher_width // 2 // CHUNKS
    unscale = HEADS * math.sqrt(DS // HEADS)
    chunks = range(CHUNKS)

    def weight_piece(owner):
        start = (my_dp * piece_rows, owner * my_width)
        return lax.dynamic_slice(out_proj, start, (piece_rows, my_width))

    kept, sent = weight_piece(place), weight_piece(1 - place)
    swapped = swap(sent, "ctx", 1)

    pieces = split(after(tokens, kept, sent), n_ctx, n_dp)

    def piece(owner):
        return lax.dynamic_index_in_dim(pieces, owner, 0, keepdims=False)

    documents = [piece(my_dp)]
    for steps in range(1, n_dp):
        documents.append(rotate(piece(lax.rem(my_dp + steps, n_dp)), "dp", steps))
    others = [swap(rows, "ctx", 1) for rows in documents]
    pair = jnp.concatenate(ordered(kept, after(swapped, documents[-1]), place), 0)

    def teacher_columns(owner, chunk):
        starts = [
            owner * teacher_width + (half * CHUNKS + chunk) * teacher_chunk for half in range(2)
        ]
        partial = after(teacher_part, kept, sent)[0, 0]
        return [lax.dynamic_slice_in_dim(partial, start, teacher_chunk, 1) for start in starts]

    kept_columns, left_columns = [], []
    for chunk in chunks:
        total = [part.astype(jnp.float32) for part in teacher_columns(my_tp, chunk)]
        for steps in range(1, n_tp):
            leaving = jnp.concatenate(teacher_columns(lax.rem(my_tp + steps, n_tp), chunk), 1)
            arrived = rotate(after(leaving, pair) if chunk else leaving, "tp", steps)
            if chunk:
                arrived = after(arrived, kept_columns[-1], left_columns[-1])
            total = [
                t + arrived[:, half * teacher_chunk : (half + 1) * teacher_chunk].astype(jnp.float32)
                for half, t in enumerate(total)
            ]
        mine, other = ordered(*[t.astype(jnp.bfloat16) for t in total], place)
        kept_columns.append(mine)
        left_columns.append(other)

    teacher, turned = [], []
    for mine, other in zip(kept_columns, left_columns):
        if turned:
            other = after(other, turned[-1])
        turned.append(swap(other, "ctx", 1))
        teacher.append(ordered(mine, turned[-1], place))

    gates = {
        2: (others[0], left_columns[0]),
        groups - 1: (*others, left_columns[-1], turned[0]),
    }
    weights = gather_line(pair, "ctx", gates)
    rows = [jnp.concatenate(pair_of, 0) for pair_of in zip(documents, others)]
    rows_turned = row_major(jnp.concatenate(rows, 0).T)
    weights[-1] = (weights[-1][0], after(weights[-1][1], rows_turned, turned[-1]))

    def project(document):
        product = 0.0
        for source, block in weights:
            inputs = lax.dynamic_slice_in_dim(
                rows[document], source * (2 * piece_rows), 2 * piece_rows, 1
            )
            product = product + jnp.dot(inputs, block, preferred_element_type=jnp.float32)
        return product

    total = 0.0
    for steps in range(1, n_dp):
        total = total + rotate(project(steps), "dp", -steps)
    total = (project(0) + total).astype(jnp.bfloat16)
    student = ordered(total[:length], total[length:], place)

    valid = valid_count[0]
    padded = jnp.concatenate([jnp.full((length,), -1, jnp.int32), segment_ids[0]], 0)
    start = group * (2 * length)
    segments = lax.dynamic_slice_in_dim(padded, start, 3 * length, 0)
    position = start - length + jnp.arange(3 * length, dtype=jnp.int32)
    segments_kept = jnp.where(position < valid, segments, -2)
    allowed = [
        segments_kept[w * length : (w + 2) * length, None]
        == segments[None, (w + 1) * length : (w + 2) * length]
        for w in range(2)
    ]
    bias = jnp.where(jnp.stack(allowed), 0.0, MASKED).astype(jnp.float32)
    live = jnp.where(position[length:] < valid, 1.0, 0.0).astype(jnp.float32)
    live = live.reshape(2, 1, length)

    results = []
    for chunk in chunks:
        columns = slice(chunk * chunk_width, (chunk + 1) * chunk_width)
        states = [half[:, columns] for half in student]
        leaving = teacher[chunk][1]
        teacher_past = shift(after(leaving, total) if chunk else leaving, "ctx", 2)
        states = (shift(after(states[1], teacher_past), "ctx", 2), *states)
        if results:
            live = after(live, results[-1][0])
        results.append(attention((teacher_past, *teacher[chunk]), states, bias, live))

    parts, state_grad, beside = [], [], ()
    for _, grad_past, grad_first, grad_second in results:
        from_next = shift(grad_past, "ctx", -2).astype(jnp.float32)
        grad_second = (grad_second + from_next).astype(jnp.bfloat16)
        mine, other = ordered(grad_first, grad_second, place)
        block = jnp.concatenate([mine, other], 0)
        blocks = [block] + [rotate(block, "dp", steps) for steps in range(1, n_dp)]
        product = jnp.dot(
            rows_turned, jnp.concatenate(blocks, 0), preferred_element_type=jnp.float32
        )
        total, beside = scatter_line(product.reshape(groups, 2 * piece_rows, chunk_width), "ctx")
        state_grad.append(ordered(mine, swap(after(other, blocks[-1]), "ctx", 1), place))

        total = total.astype(jnp.bfloat16)
        mine = lax.dynamic_slice_in_dim(total, place * piece_rows, piece_rows, 0)
        other = lax.dynamic_slice_in_dim(total, (1 - place) * piece_rows, piece_rows, 0)
        total = jnp.concatenate(ordered(mine, swap(other, "ctx", 1), place), 1)
        owners = [total] + [rotate(total, "dp", steps) for steps in range(1, n_dp)]
        parts.append(jnp.concatenate(by_owner(owners, my_dp), 0))

    halves = [slice(half * chunk_width, (half + 1) * chunk_width) for half in range(2)]
    wo_grad = jnp.concatenate([part[:, half] for half in halves for part in parts], 1)
    state_grad = jnp.concatenate([pair[half] for half in range(2) for pair in state_grad], 1)
    state_grad = state_grad.astype(jnp.float32) * unscale

    doc_loss = sum(jnp.sum(loss) for loss, *_ in results) / HEADS
    doc_loss = jnp.broadcast_to(doc_loss, (1, 128))
    steps = [("tp", 1 << bit) for bit in range(n_tp.bit_length() - 1)]
    steps += [("ctx", 1 << bit) for bit in range(n_ctx.bit_length() - 1)]
    for axis, distance in steps:
        if axis == "ctx" and distance > 1:
            doc_loss = after(doc_loss, *beside)
        doc_loss = doc_loss + swap(doc_loss, axis, distance)
    return (doc_loss[0, :1], wo_grad.astype(jnp.float32), state_grad[None])


def solution(mesh):
    return jax.shard_map(
        per_device,
        mesh=mesh,
        in_specs=(
            P("dp", "tp", "ctx", None),
            P("dp", "ctx", None),
            P("ctx", "tp"),
            P("dp", None),
            P("dp"),
        ),
        out_specs=(P("dp"), P("ctx", "tp"), P("dp", "ctx", "tp")),
        check_vma=False,
    )
```

time: 723 us -> 259 us (0.36)
  waiting for transfers between devices: 558 us -> 98.9 us
  starting transfers between devices: 8.33 us -> 83.8 us
  blocking collectives: 34.2 us -> 0 us
  matrix products: 41.9 us -> 20.4 us
  between operations: 16.9 us -> 3.29 us
  Pallas kernels: 0 us -> 12.4 us
  local copies, waits for them, and re-layouts: 22.9 us -> 11.7 us
    reduce_scatter x2 -> x0, waiting for transfers between devices: 338 us -> none  [the longest x1 282 us: per_device(): lax.psum_scatter(jnp.einsum('tr,tc->rc', columns, hidden_grad, preferred_...]
    all_gather x1 -> x0, waiting for transfers between devices: 160 us -> none  [per_device(): lax.all_gather(out_proj, 'ctx', axis=0, tiled=True)]
    ppermute x3 -> x42, starting transfers between devices: 8.17 us -> 83.8 us  [the longest x15 36.1 us: send_line(): return lax.ppermute(value, axis, pairs)]
    ppermute x3 -> x42, waiting for transfers between devices: 59.1 us -> 98.9 us  [the longest x15 55.6 us: send_line(): return lax.ppermute(value, axis, pairs)]
    psum x1 -> x0, blocking collectives: 34.2 us -> none  [per_device(): doc_loss = lax.psum(loss_part, ('ctx', 'tp'))]
    reduce_sum x3 -> x2, other arithmetic: 21.8 us -> 1.26 us  [per_device(): doc_loss = sum((jnp.sum(loss) for loss, *_ in results)) / HEADS]
    sub x2 -> x0, matrix products: 15.9 us -> none  [log_probs(): shifted = scores - top]
    pallas_call x0 -> x3, Pallas kernels: none -> 12.4 us  [the longest x2 11.8 us: attention(): pl.pallas_call(kernel, grid=(steps,), in_specs=[inputs(dt)] * 3 + [inputs...]
  transfers between devices with their start and end apart: 7 -> 42, of which waited for: 6 -> 19; matrix products, arithmetic and copies ran while one was open for 5% -> 19% of each run, Pallas kernels for 0% -> 5%
where the time goes in v1:
time: 259 us; the launch traced here: 258 us
  waiting for transfers between devices  98.9 us (38%)
  starting transfers between devices  83.8 us (32%)
  other arithmetic  27.3 us (11%)
  matrix products  20.4 us (8%)
  Pallas kernels  12.4 us (5%)
  local copies, waits for them, and re-layouts  11.7 us (5%)
  between operations  3.29 us (1%)
    ppermute x15, waiting for transfers between devices, send_line(): return lax.ppermute(value, axis, pairs)  55.6 us
    ppermute x15, starting transfers between devices, send_line(): return lax.ppermute(value, axis, pairs)  36.1 us
    ppermute x13, waiting for transfers between devices, swap(): return lax.ppermute(value, axis, [(i, i ^ distance) for i in range(count)])  27.2 us
    ppermute x6, starting transfers between devices, shift(): return lax.ppermute(value, axis, pairs)  16.9 us
    ppermute x8, starting transfers between devices, rotate(): lax.ppermute(value, axis, [(i, (i + steps) % count) for i in range(count)])  15.4 us
    ppermute x13, starting transfers between devices, swap(): return lax.ppermute(value, axis, [(i, i ^ distance) for i in range(count)])  15.3 us
    dot_general x10, matrix products, project(): jnp.dot(inputs, block, preferred_element_type=jnp.float32)  12.5 us
    pallas_call x2, Pallas kernels, attention(): pl.pallas_call(kernel, grid=(steps,), in_specs=[inputs(dt)] * 3 + [inputs...  11.8 us
  transfers between devices with their start and end apart: 42, of which 19 were waited for; matrix products, arithmetic and copies ran while one was open for 19% of the time, Pallas kernels for 5%

profile of v1, /device:TPU:1, one launch (start us, length us, event | category | flops | bytes accessed | tf_op | source)
XLA Modules:
  0.0 257.8 jit_solution(8819039673760831613)
XLA Ops:
  6.4 2.7 %collective-permute-start.4 = (bf16[256,1024]{1,0:T(8,128)(2,1)}, bf16[256,1024]{1,0:T(8,128)(2,1)}, u32[]{:S(2)}, u32[]{:S(2)}) collective-permute-start(bf16[256,1024]{1,0:T(8,128)(2,1)} %get-tuple-element.76), channel_id=1, source_target_pairs={{0,2},{2,0},{4,6},{6,4},{8,10},{10,8},{12,14},{14,12},{1,3},{3,1},... | collective-permute-start | bytes 1572872 | tf_op jit(solution)/shard_map/ppermute | solution.py:34
  9.1 2.7 %dynamic-slice_bitcast_fusion.1 = (bf16[256,1024]{1,0:T(8,128)(2,1)}, bf16[256,1024]{1,0:T(8,128)(2,1)}, bf16[256,1024]{1,0:T(8,128)(2,1)S(1)}, bf16[256,1024]{1,0:T(8,128)(2,1)S(1)}) fusion(bf16[1,1,256,8192]{3,2,1,0:T(8,128)(2,1)} %param.5, s32[]{:T(128)S(6)} %select_n.303, s32[]{:T(128)S(6)} %select_n.304, s32[]{:T(128)S(6)} %select_n.283, s32[]{:T(128)S(6)} %select_n.282), kind=kLoop, calls=%fused_computation.114 | loop fusion | bytes 4194320 | tf_op jit(solution)/shard_map/dynamic_slice | solution.py:282
  15.6 6.0 %collective-permute-done.4 = bf16[256,1024]{1,0:T(8,128)(2,1)} collective-permute-done((bf16[256,1024]{1,0:T(8,128)(2,1)}, bf16[256,1024]{1,0:T(8,128)(2,1)}, u32[]{:S(2)}, u32[]{:S(2)}) %collective-permute-start.4) | collective-permute-done | bytes 524320 | tf_op jit(solution)/shard_map/ppermute | solution.py:34
  23.9 4.2 %collective-permute-start.6 = (bf16[512,1024]{1,0:T(8,128)(2,1)}, bf16[512,1024]{1,0:T(8,128)(2,1)}, u32[]{:S(2)}, u32[]{:S(2)}) collective-permute-start(bf16[512,1024]{1,0:T(8,128)(2,1)} %pad_maximum_fusion.1), channel_id=1, source_target_pairs={{0,4},{2,6},{4,8},{6,10},{8,12},{10,14},{1,5},{3,7},{5,9},{7,11},{... | collective-permute-start | bytes 3145736 | tf_op jit(solution)/shard_map/ppermute | solution.py:52
  31.9 5.8 %collective-permute-done = bf16[256,2048]{1,0:T(8,128)(2,1)} collective-permute-done((bf16[256,2048]{1,0:T(8,128)(2,1)}, bf16[256,2048]{1,0:T(8,128)(2,1)}, u32[]{:S(2)}, u32[]{:S(2)}) %collective-permute-start) | collective-permute-done | bytes 1048608 | tf_op jit(solution)/shard_map/ppermute | solution.py:29
  40.5 3.6 %collective-permute-done.3 = bf16[256,2048]{0,1:T(8,128)(2,1)S(1)} collective-permute-done((bf16[256,2048]{0,1:T(8,128)(2,1)S(1)}, bf16[256,2048]{0,1:T(8,128)(2,1)S(1)}, u32[]{:S(2)}, u32[]{:S(2)}) %collective-permute-start.3) | collective-permute-done | bytes 1048608 | tf_op jit(solution)/shard_map/ppermute | solution.py:34
  45.4 3.2 %collective-permute-done.6 = bf16[512,1024]{1,0:T(8,128)(2,1)} collective-permute-done((bf16[512,1024]{1,0:T(8,128)(2,1)}, bf16[512,1024]{1,0:T(8,128)(2,1)}, u32[]{:S(2)}, u32[]{:S(2)}) %collective-permute-start.6) | collective-permute-done | bytes 1048608 | tf_op jit(solution)/shard_map/ppermute | solution.py:52
  49.3 4.1 %collective-permute-done.7 = bf16[512,1024]{1,0:T(8,128)(2,1)} collective-permute-done((bf16[512,1024]{1,0:T(8,128)(2,1)}, bf16[512,1024]{1,0:T(8,128)(2,1)}, u32[]{:S(2)}, u32[]{:S(2)}) %collective-permute-start.7) | collective-permute-done | bytes 1048608 | tf_op jit(solution)/shard_map/ppermute | solution.py:52
  62.3 14.6 %collective-permute-done.10 = bf16[256,2048]{0,1:T(8,128)(2,1)} collective-permute-done((bf16[256,2048]{0,1:T(8,128)(2,1)}, bf16[256,2048]{0,1:T(8,128)(2,1)}, u32[]{:S(2)}, u32[]{:S(2)}) %collective-permute-start.10) | collective-permute-done | bytes 1048608 | tf_op jit(solution)/shard_map/ppermute | solution.py:34
  85.1 2.9 %collective-permute-done.13 = bf16[256,1024]{1,0:T(8,128)(2,1)S(1)} collective-permute-done((bf16[256,1024]{1,0:T(8,128)(2,1)S(1)}, bf16[256,1024]{1,0:T(8,128)(2,1)S(1)}, u32[]{:S(2)}, u32[]{:S(2)}) %collective-permute-start.13) | collective-permute-done | bytes 524320 | tf_op jit(solution)/shard_map/ppermute | solution.py:34
  88.0 13.9 %collective-permute-done.12 = bf16[512,1024]{1,0:T(8,128)(2,1)S(1)} collective-permute-done((bf16[512,1024]{1,0:T(8,128)(2,1)S(1)}, bf16[512,1024]{1,0:T(8,128)(2,1)S(1)}, u32[]{:S(2)}, u32[]{:S(2)}) %collective-permute-start.12) | collective-permute-done | bytes 1048608 | tf_op jit(solution)/shard_map/ppermute | solution.py:52
  102.7 4.0 %collective-permute-start.14 = (f32[512,1024]{1,0:T(8,128)S(1)}, f32[512,1024]{1,0:T(8,128)S(1)}, u32[]{:S(2)}, u32[]{:S(2)}) collective-permute-start(f32[512,1024]{1,0:T(8,128)S(1)} %add_add_fusion), channel_id=1, source_target_pairs={{0,16},{16,0},{1,17},{17,1},{2,18},{18,2},{3,19},{19,3},{4,20},{20... | collective-permute-start | bytes 6291464 | tf_op jit(solution)/shard_map/ppermute | solution.py:29
  117.5 4.4 %collective-permute-start.16 = (bf16[256,1024]{1,0:T(8,128)(2,1)S(1)}, bf16[256,1024]{1,0:T(8,128)(2,1)S(1)}, u32[]{:S(2)}, u32[]{:S(2)}) collective-permute-start(bf16[256,1024]{1,0:T(8,128)(2,1)S(1)} %get-tuple-element.41.refs_2_), channel_id=1, source_target_pairs={{0,4},{2,6},{4,8},{6,10},{8,12},{10,14},{1,5},{3,7},{5,9},{7,11},{... | collective-permute-start | bytes 1572872 | tf_op jit(solution)/shard_map/ppermute | solution.py:40
  122.1 4.1 %collective-permute-start.15 = (bf16[256,512]{1,0:T(8,128)(2,1)S(1)}, bf16[256,512]{1,0:T(8,128)(2,1)S(1)}, u32[]{:S(2)}, u32[]{:S(2)}) collective-permute-start(bf16[256,512]{1,0:T(8,128)(2,1)S(1)} %get-tuple-element.39.refs_5_), channel_id=1, source_target_pairs={{0,4},{2,6},{4,8},{6,10},{8,12},{10,14},{1,5},{3,7},{5,9},{7,11},{... | collective-permute-start | bytes 786440 | tf_op jit(solution)/shard_map/ppermute | solution.py:40
  126.3 6.7 %collective-permute-done.16.refs_0_ = bf16[256,1024]{1,0:T(8,128)(2,1)S(1)} collective-permute-done((bf16[256,1024]{1,0:T(8,128)(2,1)S(1)}, bf16[256,1024]{1,0:T(8,128)(2,1)S(1)}, u32[]{:S(2)}, u32[]{:S(2)}) %collective-permute-start.16) | collective-permute-done | bytes 524320 | tf_op jit(solution)/shard_map/ppermute | solution.py:40
  133.0 4.1 %collective-permute-start.17 = (bf16[256,512]{1,0:T(8,128)(2,1)S(1)}, bf16[256,512]{1,0:T(8,128)(2,1)S(1)}, u32[]{:S(2)}, u32[]{:S(2)}) collective-permute-start(bf16[256,512]{1,0:T(8,128)(2,1)S(1)} %get-tuple-element.42.refs_5_), channel_id=1, source_target_pairs={{0,4},{2,6},{4,8},{6,10},{8,12},{10,14},{1,5},{3,7},{5,9},{7,11},{... | collective-permute-start | bytes 786440 | tf_op jit(solution)/shard_map/ppermute | solution.py:40
  138.6 5.9 %window_attention.2 = (f32[1,256]{1,0:T(1,128)S(1)}, bf16[256,512]{1,0:T(8,128)(2,1)S(1)}, bf16[256,512]{1,0:T(8,128)(2,1)S(1)}, f32[256,512]{1,0:T(8,128)S(1)}) custom-call(bf16[256,1024]{1,0:T(8,128)(2,1)S(1)} %collective-permute-done.2.refs_0_, bf16[256,1024]{1,0:T(8,128)(2,1)S(1)} %get-tuple-element.60.refs_1_, ...), custom_call_target="tpu_custom_call" | custom-call | flops 1342177280 | bytes 3407872 | tf_op jit(solution)/shard_map/window_attention/pallas_call | solution.py:222
  145.8 5.9 %window_attention.3 = (f32[1,256]{1,0:T(1,128)S(1)}, bf16[256,512]{1,0:T(8,128)(2,1)S(1)}, bf16[256,512]{1,0:T(8,128)(2,1)S(1)}, f32[256,512]{1,0:T(8,128)S(1)}) custom-call(bf16[256,1024]{1,0:T(8,128)(2,1)S(1)} %collective-permute-done.16.refs_0_, bf16[256,1024]{1,0:T(8,128)(2,1)S(1)} %get-tuple-element.78.refs_1_, ...), custom_call_target="tpu_custom_call" | custom-call | flops 1342177280 | bytes 3407872 | tf_op jit(solution)/shard_map/window_attention/pallas_call | solution.py:222
  165.0 4.0 %fusion.16 = f32[2048,512]{1,0:T(8,128)S(1)} fusion(bf16[512,512]{1,0:T(8,128)(2,1)} %collective-permute-done.30, bf16[256,512]{1,0:T(8,128)(2,1)S(1)} %copy-done.4, bf16[256,512]{1,0:T(8,128)(2,1)S(1)} %get-tuple-element.82, bf16[256,2048]{0,1:T(8,128)(2,1)} %collective-permute-done.10, bf16[256,2048]{0,1:T(8,128)(2,1)} %collective-permute-done.5, ...), kind=kOutput, calls=%fused_computation.36 | convolution fusion | flops 2167406592 | bytes 9437184 | tf_op jit(solution)/shard_map/dot_general | solution.py:364
  169.2 4.3 %collective-permute-start.31 = (bf16[512,512]{1,0:T(8,128)(2,1)S(1)}, bf16[512,512]{1,0:T(8,128)(2,1)S(1)}, u32[]{:S(2)}, u32[]{:S(2)}) collective-permute-start(bf16[512,512]{1,0:T(8,128)(2,1)S(1)} %fusion.41), channel_id=1, source_target_pairs={{0,4},{2,6},{12,8},{14,10},{1,5},{3,7},{13,9},{15,11},{16,20},{18,... | collective-permute-start | bytes 1572872 | tf_op jit(solution)/shard_map/ppermute | solution.py:52
  173.5 3.9 %fusion.10 = f32[2048,512]{1,0:T(8,128)S(1)} fusion(bf16[512,512]{1,0:T(8,128)(2,1)S(1)} %collective-permute-done.21, bf16[256,512]{1,0:T(8,128)(2,1)S(1)} %get-tuple-element.54, bf16[256,512]{1,0:T(8,128)(2,1)S(1)} %get-tuple-element.86, bf16[256,2048]{0,1:T(8,128)(2,1)} %collective-permute-done.10, bf16[256,2048]{0,1:T(8,128)(2,1)} %collective-permute-done.5, ...), kind=kOutput, calls=%fused_computation.30 | convolution fusion | flops 2167406592 | bytes 9437184 | tf_op jit(solution)/shard_map/dot_general | solution.py:364
  179.8 4.9 %collective-permute-done.31 = bf16[512,512]{1,0:T(8,128)(2,1)S(1)} collective-permute-done((bf16[512,512]{1,0:T(8,128)(2,1)S(1)}, bf16[512,512]{1,0:T(8,128)(2,1)S(1)}, u32[]{:S(2)}, u32[]{:S(2)}) %collective-permute-start.31) | collective-permute-done | bytes 524320 | tf_op jit(solution)/shard_map/ppermute | solution.py:52
  185.1 4.1 %collective-permute-start.32 = (bf16[512,512]{1,0:T(8,128)(2,1)S(1)}, bf16[512,512]{1,0:T(8,128)(2,1)S(1)}, u32[]{:S(2)}, u32[]{:S(2)}) collective-permute-start(bf16[512,512]{1,0:T(8,128)(2,1)S(1)} %get-tuple-element.62), channel_id=1, source_target_pairs={{0,4},{2,6},{4,8},{6,10},{1,5},{3,7},{5,9},{7,11},{16,20},{18,22},... | collective-permute-start | bytes 1572872 | tf_op jit(solution)/shard_map/ppermute | solution.py:52
  190.9 5.0 %collective-permute-done.22 = bf16[512,512]{1,0:T(8,128)(2,1)S(1)} collective-permute-done((bf16[512,512]{1,0:T(8,128)(2,1)S(1)}, bf16[512,512]{1,0:T(8,128)(2,1)S(1)}, u32[]{:S(2)}, u32[]{:S(2)}) %collective-permute-start.22) | collective-permute-done | bytes 524320 | tf_op jit(solution)/shard_map/ppermute | solution.py:52
  197.0 4.7 %collective-permute-start.23 = (bf16[512,512]{1,0:T(8,128)(2,1)S(1)}, bf16[512,512]{1,0:T(8,128)(2,1)S(1)}, u32[]{:S(2)}, u32[]{:S(2)}) collective-permute-start(bf16[512,512]{1,0:T(8,128)(2,1)S(1)} %get-tuple-element.65), channel_id=1, source_target_pairs={{0,4},{2,6},{4,8},{6,10},{1,5},{3,7},{5,9},{7,11},{16,20},{18,22},... | collective-permute-start | bytes 1572872 | tf_op jit(solution)/shard_map/ppermute | solution.py:52
  202.8 4.4 %collective-permute-done.32 = bf16[512,512]{1,0:T(8,128)(2,1)S(1)} collective-permute-done((bf16[512,512]{1,0:T(8,128)(2,1)S(1)}, bf16[512,512]{1,0:T(8,128)(2,1)S(1)}, u32[]{:S(2)}, u32[]{:S(2)}) %collective-permute-start.32) | collective-permute-done | bytes 524320 | tf_op jit(solution)/shard_map/ppermute | solution.py:52
  208.9 4.8 %collective-permute-start.33 = (bf16[512,512]{1,0:T(8,128)(2,1)S(1)}, bf16[512,512]{1,0:T(8,128)(2,1)S(1)}, u32[]{:S(2)}, u32[]{:S(2)}) collective-permute-start(bf16[512,512]{1,0:T(8,128)(2,1)S(1)} %get-tuple-element.66), channel_id=1, source_target_pairs={{0,4},{2,6},{4,8},{6,10},{8,12},{10,14},{1,5},{3,7},{5,9},{7,11},{... | collective-permute-start | bytes 1572872 | tf_op jit(solution)/shard_map/ppermute | solution.py:52
  213.7 4.7 %collective-permute-done.23 = bf16[512,512]{1,0:T(8,128)(2,1)S(1)} collective-permute-done((bf16[512,512]{1,0:T(8,128)(2,1)S(1)}, bf16[512,512]{1,0:T(8,128)(2,1)S(1)}, u32[]{:S(2)}, u32[]{:S(2)}) %collective-permute-start.23) | collective-permute-done | bytes 524320 | tf_op jit(solution)/shard_map/ppermute | solution.py:52
  218.8 4.1 %collective-permute-start.24 = (bf16[512,512]{1,0:T(8,128)(2,1)S(1)}, bf16[512,512]{1,0:T(8,128)(2,1)S(1)}, u32[]{:S(2)}, u32[]{:S(2)}) collective-permute-start(bf16[512,512]{1,0:T(8,128)(2,1)S(1)} %get-tuple-element.69), channel_id=1, source_target_pairs={{0,4},{2,6},{4,8},{6,10},{8,12},{10,14},{1,5},{3,7},{5,9},{7,11},{... | collective-permute-start | bytes 1572872 | tf_op jit(solution)/shard_map/ppermute | solution.py:52
  224.3 5.3 %collective-permute-done.33 = bf16[512,512]{1,0:T(8,128)(2,1)S(1)} collective-permute-done((bf16[512,512]{1,0:T(8,128)(2,1)S(1)}, bf16[512,512]{1,0:T(8,128)(2,1)S(1)}, u32[]{:S(2)}, u32[]{:S(2)}) %collective-permute-start.33) | collective-permute-done | bytes 524320 | tf_op jit(solution)/shard_map/ppermute | solution.py:52
  231.0 10.0 %collective-permute-done.24 = bf16[512,512]{1,0:T(8,128)(2,1)S(1)} collective-permute-done((bf16[512,512]{1,0:T(8,128)(2,1)S(1)}, bf16[512,512]{1,0:T(8,128)(2,1)S(1)}, u32[]{:S(2)}, u32[]{:S(2)}) %collective-permute-start.24) | collective-permute-done | bytes 524320 | tf_op jit(solution)/shard_map/ppermute | solution.py:52
  253.6 4.2 %fusion.8 = f32[512,2048]{1,0:T(8,128)} fusion(bf16[256,1024]{1,0:T(8,128)(2,1)S(1)} %get-tuple-element.85, bf16[256,1024]{1,0:T(8,128)(2,1)S(1)} %get-tuple-element.84, bf16[256,1024]{1,0:T(8,128)(2,1)S(1)} %get-tuple-element.81, bf16[256,1024]{1,0:T(8,128)(2,1)S(1)} %get-tuple-element.80, bf16[512,512]{1,0:T(8,128)(2,1)S(1)} %fusion.42, ...), kind=kLoop, calls=%fused_computation.22 | loop fusion | flops 20971520 | bytes 7340032 | tf_op jit(solution)/shard_map/convert_element_type | solution.py:390
  (140 shorter events, 87.2 us)
Async XLA Ops:
  6.3 15.3 %collective-permute-start.5 = (bf16[256,2048]{0,1:T(8,128)(2,1)S(1)}, bf16[256,2048]{0,1:T(8,128)(2,1)}, u32[]{:S(2)}, u32[]{:S(2)}) collective-permute-start(bf16[256,2048]{0,1:T(8,128)(2,1)S(1)} %bitcast.128), channel_id=1, source_target_pairs={{0,16},{16,0},{1,17},{17,1},{2,18},{18,2},{3,19},{19,3},{4,20},{20... | collective-permute-start | bytes 3145736 | tf_op jit(solution)/shard_map/ppermute | solution.py:29
  6.4 15.2 %collective-permute-start.4 = (bf16[256,1024]{1,0:T(8,128)(2,1)}, bf16[256,1024]{1,0:T(8,128)(2,1)}, u32[]{:S(2)}, u32[]{:S(2)}) collective-permute-start(bf16[256,1024]{1,0:T(8,128)(2,1)} %get-tuple-element.76), channel_id=1, source_target_pairs={{0,2},{2,0},{4,6},{6,4},{8,10},{10,8},{12,14},{14,12},{1,3},{3,1},... | collective-permute-start | bytes 1572872 | tf_op jit(solution)/shard_map/ppermute | solution.py:34
  12.9 24.7 %collective-permute-start = (bf16[256,2048]{1,0:T(8,128)(2,1)}, bf16[256,2048]{1,0:T(8,128)(2,1)}, u32[]{:S(2)}, u32[]{:S(2)}) collective-permute-start(bf16[256,2048]{1,0:T(8,128)(2,1)} %pad_maximum_fusion), channel_id=1, source_target_pairs={{0,1},{1,0},{2,3},{3,2},{4,5},{5,4},{6,7},{7,6},{8,9},{9,8},{10,11... | collective-permute-start | bytes 3145736 | tf_op jit(solution)/shard_map/ppermute | solution.py:29
  14.6 29.5 %collective-permute-start.3 = (bf16[256,2048]{0,1:T(8,128)(2,1)S(1)}, bf16[256,2048]{0,1:T(8,128)(2,1)S(1)}, u32[]{:S(2)}, u32[]{:S(2)}) collective-permute-start(bf16[256,2048]{0,1:T(8,128)(2,1)S(1)} %bitcast.112), channel_id=1, source_target_pairs={{0,2},{2,0},{4,6},{6,4},{8,10},{10,8},{12,14},{14,12},{1,3},{3,1},... | collective-permute-start | bytes 3145736 | tf_op jit(solution)/shard_map/ppermute | solution.py:34
  23.9 24.7 %collective-permute-start.6 = (bf16[512,1024]{1,0:T(8,128)(2,1)}, bf16[512,1024]{1,0:T(8,128)(2,1)}, u32[]{:S(2)}, u32[]{:S(2)}) collective-permute-start(bf16[512,1024]{1,0:T(8,128)(2,1)} %pad_maximum_fusion.1), channel_id=1, source_target_pairs={{0,4},{2,6},{4,8},{6,10},{8,12},{10,14},{1,5},{3,7},{5,9},{7,11},{... | collective-permute-start | bytes 3145736 | tf_op jit(solution)/shard_map/ppermute | solution.py:52
  28.2 25.3 %collective-permute-start.7 = (bf16[512,1024]{1,0:T(8,128)(2,1)}, bf16[512,1024]{1,0:T(8,128)(2,1)}, u32[]{:S(2)}, u32[]{:S(2)}) collective-permute-start(bf16[512,1024]{1,0:T(8,128)(2,1)} %pad_maximum_fusion.1), channel_id=1, source_target_pairs={{4,0},{6,2},{8,4},{10,6},{12,8},{14,10},{5,1},{7,3},{9,5},{11,7},{... | collective-permute-start | bytes 3145736 | tf_op jit(solution)/shard_map/ppermute | solution.py:52
  30.6 29.4 %collective-permute-start.11 = (bf16[256,2048]{1,0:T(8,128)(2,1)}, bf16[256,2048]{1,0:T(8,128)(2,1)}, u32[]{:S(2)}, u32[]{:S(2)}) collective-permute-start(bf16[256,2048]{1,0:T(8,128)(2,1)} %pad_maximum_fusion.2), channel_id=1, source_target_pairs={{0,1},{1,0},{2,3},{3,2},{4,5},{5,4},{6,7},{7,6},{8,9},{9,8},{10,11... | collective-permute-start | bytes 3145736 | tf_op jit(solution)/shard_map/ppermute | solution.py:29
  40.3 15.8 %collective-permute-start.1 = (bf16[256,1024]{1,0:T(8,128)(2,1)}, bf16[256,1024]{1,0:T(8,128)(2,1)}, u32[]{:S(2)}, u32[]{:S(2)}) collective-permute-start(bf16[256,1024]{1,0:T(8,128)(2,1)} %broadcast_select_fusion.16), channel_id=1, source_target_pairs={{0,2},{2,0},{4,6},{6,4},{8,10},{10,8},{12,14},{14,12},{1,3},{3,1},... | collective-permute-start | bytes 1572872 | tf_op jit(solution)/shard_map/ppermute | solution.py:34
  44.1 32.8 %collective-permute-start.10 = (bf16[256,2048]{0,1:T(8,128)(2,1)}, bf16[256,2048]{0,1:T(8,128)(2,1)}, u32[]{:S(2)}, u32[]{:S(2)}) collective-permute-start(bf16[256,2048]{0,1:T(8,128)(2,1)} %collective-permute-done.5), channel_id=1, source_target_pairs={{0,2},{2,0},{4,6},{6,4},{8,10},{10,8},{12,14},{14,12},{1,3},{3,1},... | collective-permute-start | bytes 3145736 | tf_op jit(solution)/shard_map/ppermute | solution.py:34
  48.6 29.6 %collective-permute-start.8 = (bf16[512,1024]{1,0:T(8,128)(2,1)}, bf16[512,1024]{1,0:T(8,128)(2,1)S(1)}, u32[]{:S(2)}, u32[]{:S(2)}) collective-permute-start(bf16[512,1024]{1,0:T(8,128)(2,1)} %collective-permute-done.6), channel_id=1, source_target_pairs={{4,8},{6,10},{8,12},{10,14},{5,9},{7,11},{9,13},{11,15},{20,24},{2... | collective-permute-start | bytes 3145736 | tf_op jit(solution)/shard_map/ppermute | solution.py:52
  53.4 24.8 %collective-permute-start.9 = (bf16[512,1024]{1,0:T(8,128)(2,1)}, bf16[512,1024]{1,0:T(8,128)(2,1)S(1)}, u32[]{:S(2)}, u32[]{:S(2)}) collective-permute-start(bf16[512,1024]{1,0:T(8,128)(2,1)} %collective-permute-done.7), channel_id=1, source_target_pairs={{4,0},{6,2},{8,4},{10,6},{5,1},{7,3},{9,5},{11,7},{20,16},{22,18},... | collective-permute-start | bytes 3145736 | tf_op jit(solution)/shard_map/ppermute | solution.py:52
  62.0 26.0 %collective-permute-start.13 = (bf16[256,1024]{1,0:T(8,128)(2,1)S(1)}, bf16[256,1024]{1,0:T(8,128)(2,1)S(1)}, u32[]{:S(2)}, u32[]{:S(2)}) collective-permute-start(bf16[256,1024]{1,0:T(8,128)(2,1)S(1)} %get-tuple-element.37), channel_id=1, source_target_pairs={{0,2},{2,0},{4,6},{6,4},{8,10},{10,8},{12,14},{14,12},{1,3},{3,1},... | collective-permute-start | bytes 1572872 | tf_op jit(solution)/shard_map/ppermute | solution.py:34
  78.3 23.5 %collective-permute-start.12 = (bf16[512,1024]{1,0:T(8,128)(2,1)S(1)}, bf16[512,1024]{1,0:T(8,128)(2,1)S(1)}, u32[]{:S(2)}, u32[]{:S(2)}) collective-permute-start(bf16[512,1024]{1,0:T(8,128)(2,1)S(1)} %broadcast_select_fusion), channel_id=1, source_target_pairs={{8,12},{10,14},{4,0},{6,2},{9,13},{11,15},{5,1},{7,3},{24,28},{26,... | collective-permute-start | bytes 3145736 | tf_op jit(solution)/shard_map/ppermute | solution.py:52
  102.7 13.3 %collective-permute-start.14 = (f32[512,1024]{1,0:T(8,128)S(1)}, f32[512,1024]{1,0:T(8,128)S(1)}, u32[]{:S(2)}, u32[]{:S(2)}) collective-permute-start(f32[512,1024]{1,0:T(8,128)S(1)} %add_add_fusion), channel_id=1, source_target_pairs={{0,16},{16,0},{1,17},{17,1},{2,18},{18,2},{3,19},{19,3},{4,20},{20... | collective-permute-start | bytes 6291464 | tf_op jit(solution)/shard_map/ppermute | solution.py:29
  108.9 13.2 %collective-permute-start.2 = (bf16[256,1024]{1,0:T(8,128)(2,1)S(1)}, bf16[256,1024]{1,0:T(8,128)(2,1)S(1)}, u32[]{:S(2)}, u32[]{:S(2)}) collective-permute-start(bf16[256,1024]{1,0:T(8,128)(2,1)S(1)} %broadcast_select_fusion.14.refs_2_), channel_id=1, source_target_pairs={{0,4},{2,6},{4,8},{6,10},{8,12},{10,14},{1,5},{3,7},{5,9},{7,11},{... | collective-permute-start | bytes 1572872 | tf_op jit(solution)/shard_map/ppermute | solution.py:40
  117.5 15.4 %collective-permute-start.16 = (bf16[256,1024]{1,0:T(8,128)(2,1)S(1)}, bf16[256,1024]{1,0:T(8,128)(2,1)S(1)}, u32[]{:S(2)}, u32[]{:S(2)}) collective-permute-start(bf16[256,1024]{1,0:T(8,128)(2,1)S(1)} %get-tuple-element.41.refs_2_), channel_id=1, source_target_pairs={{0,4},{2,6},{4,8},{6,10},{8,12},{10,14},{1,5},{3,7},{5,9},{7,11},{... | collective-permute-start | bytes 1572872 | tf_op jit(solution)/shard_map/ppermute | solution.py:40
  122.1 16.5 %collective-permute-start.15 = (bf16[256,512]{1,0:T(8,128)(2,1)S(1)}, bf16[256,512]{1,0:T(8,128)(2,1)S(1)}, u32[]{:S(2)}, u32[]{:S(2)}) collective-permute-start(bf16[256,512]{1,0:T(8,128)(2,1)S(1)} %get-tuple-element.39.refs_5_), channel_id=1, source_target_pairs={{0,4},{2,6},{4,8},{6,10},{8,12},{10,14},{1,5},{3,7},{5,9},{7,11},{... | collective-permute-start | bytes 786440 | tf_op jit(solution)/shard_map/ppermute | solution.py:40
  133.0 12.8 %collective-permute-start.17 = (bf16[256,512]{1,0:T(8,128)(2,1)S(1)}, bf16[256,512]{1,0:T(8,128)(2,1)S(1)}, u32[]{:S(2)}, u32[]{:S(2)}) collective-permute-start(bf16[256,512]{1,0:T(8,128)(2,1)S(1)} %get-tuple-element.42.refs_5_), channel_id=1, source_target_pairs={{0,4},{2,6},{4,8},{6,10},{8,12},{10,14},{1,5},{3,7},{5,9},{7,11},{... | collective-permute-start | bytes 786440 | tf_op jit(solution)/shard_map/ppermute | solution.py:40
  160.1 18.7 %collective-permute-start.18 = (f32[1,128]{1,0:T(1,128)S(1)}, f32[1,128]{1,0:T(1,128)S(1)}, u32[]{:S(2)}, u32[]{:S(2)}) collective-permute-start(f32[1,128]{1,0:T(1,128)S(1)} %broadcast_in_dim.34), channel_id=1, source_target_pairs={{0,1},{1,0},{2,3},{3,2},{4,5},{5,4},{6,7},{7,6},{8,9},{9,8},{10,11... | collective-permute-start | bytes 1544 | tf_op jit(solution)/shard_map/ppermute | solution.py:34
  169.2 15.6 %collective-permute-start.31 = (bf16[512,512]{1,0:T(8,128)(2,1)S(1)}, bf16[512,512]{1,0:T(8,128)(2,1)S(1)}, u32[]{:S(2)}, u32[]{:S(2)}) collective-permute-start(bf16[512,512]{1,0:T(8,128)(2,1)S(1)} %fusion.41), channel_id=1, source_target_pairs={{0,4},{2,6},{12,8},{14,10},{1,5},{3,7},{13,9},{15,11},{16,20},{18,... | collective-permute-start | bytes 1572872 | tf_op jit(solution)/shard_map/ppermute | solution.py:52
  177.5 18.5 %collective-permute-start.22 = (bf16[512,512]{1,0:T(8,128)(2,1)S(1)}, bf16[512,512]{1,0:T(8,128)(2,1)S(1)}, u32[]{:S(2)}, u32[]{:S(2)}) collective-permute-start(bf16[512,512]{1,0:T(8,128)(2,1)S(1)} %fusion.39), channel_id=1, source_target_pairs={{0,4},{2,6},{12,8},{14,10},{1,5},{3,7},{13,9},{15,11},{16,20},{18,... | collective-permute-start | bytes 1572872 | tf_op jit(solution)/shard_map/ppermute | solution.py:52
  185.1 22.1 %collective-permute-start.32 = (bf16[512,512]{1,0:T(8,128)(2,1)S(1)}, bf16[512,512]{1,0:T(8,128)(2,1)S(1)}, u32[]{:S(2)}, u32[]{:S(2)}) collective-permute-start(bf16[512,512]{1,0:T(8,128)(2,1)S(1)} %get-tuple-element.62), channel_id=1, source_target_pairs={{0,4},{2,6},{4,8},{6,10},{1,5},{3,7},{5,9},{7,11},{16,20},{18,22},... | collective-permute-start | bytes 1572872 | tf_op jit(solution)/shard_map/ppermute | solution.py:52
  189.2 18.0 %collective-permute-start.34 = (bf16[512,512]{1,0:T(8,128)(2,1)S(1)}, bf16[512,512]{1,0:T(8,128)(2,1)S(1)}, u32[]{:S(2)}, u32[]{:S(2)}) collective-permute-start(bf16[512,512]{1,0:T(8,128)(2,1)S(1)} %get-tuple-element.63), channel_id=1, source_target_pairs={{8,4},{10,6},{12,8},{14,10},{9,5},{11,7},{13,9},{15,11},{24,20},{2... | collective-permute-start | bytes 1572872 | tf_op jit(solution)/shard_map/ppermute | solution.py:52
  189.9 11.8 %collective-permute-start.40 = (bf16[256,512]{1,0:T(8,128)(2,1)S(1)}, bf16[256,512]{1,0:T(8,128)(2,1)S(1)}, u32[]{:S(2)}, u32[]{:S(2)}) collective-permute-start(bf16[256,512]{1,0:T(8,128)(2,1)S(1)} %copy-done.4), channel_id=1, source_target_pairs={{0,2},{2,0},{4,6},{6,4},{8,10},{10,8},{12,14},{14,12},{1,3},{3,1},... | collective-permute-start | bytes 786440 | tf_op jit(solution)/shard_map/ppermute | solution.py:34
  196.3 17.4 %collective-permute-start.25 = (bf16[512,512]{1,0:T(8,128)(2,1)S(1)}, bf16[512,512]{1,0:T(8,128)(2,1)S(1)}, u32[]{:S(2)}, u32[]{:S(2)}) collective-permute-start(bf16[512,512]{1,0:T(8,128)(2,1)S(1)} %get-tuple-element.64), channel_id=1, source_target_pairs={{8,4},{10,6},{12,8},{14,10},{9,5},{11,7},{13,9},{15,11},{24,20},{2... | collective-permute-start | bytes 1572872 | tf_op jit(solution)/shard_map/ppermute | solution.py:52
  197.0 21.4 %collective-permute-start.23 = (bf16[512,512]{1,0:T(8,128)(2,1)S(1)}, bf16[512,512]{1,0:T(8,128)(2,1)S(1)}, u32[]{:S(2)}, u32[]{:S(2)}) collective-permute-start(bf16[512,512]{1,0:T(8,128)(2,1)S(1)} %get-tuple-element.65), channel_id=1, source_target_pairs={{0,4},{2,6},{4,8},{6,10},{1,5},{3,7},{5,9},{7,11},{16,20},{18,22},... | collective-permute-start | bytes 1572872 | tf_op jit(solution)/shard_map/ppermute | solution.py:52
  201.8 22.4 %collective-permute-start.41 = (bf16[256,512]{1,0:T(8,128)(2,1)S(1)}, bf16[256,512]{1,0:T(8,128)(2,1)S(1)}, u32[]{:S(2)}, u32[]{:S(2)}) collective-permute-start(bf16[256,512]{1,0:T(8,128)(2,1)S(1)} %get-tuple-element.54), channel_id=1, source_target_pairs={{0,2},{2,0},{4,6},{6,4},{8,10},{10,8},{12,14},{14,12},{1,3},{3,1},... | collective-permute-start | bytes 786440 | tf_op jit(solution)/shard_map/ppermute | solution.py:34
  207.6 16.7 %collective-permute-start.35 = (bf16[512,512]{1,0:T(8,128)(2,1)S(1)}, bf16[512,512]{1,0:T(8,128)(2,1)S(1)}, u32[]{:S(2)}, u32[]{:S(2)}) collective-permute-start(bf16[512,512]{1,0:T(8,128)(2,1)S(1)} %get-tuple-element.67), channel_id=1, source_target_pairs={{4,0},{6,2},{8,4},{10,6},{12,8},{14,10},{5,1},{7,3},{9,5},{11,7},{... | collective-permute-start | bytes 1572872 | tf_op jit(solution)/shard_map/ppermute | solution.py:52
  208.9 20.7 %collective-permute-start.33 = (bf16[512,512]{1,0:T(8,128)(2,1)S(1)}, bf16[512,512]{1,0:T(8,128)(2,1)S(1)}, u32[]{:S(2)}, u32[]{:S(2)}) collective-permute-start(bf16[512,512]{1,0:T(8,128)(2,1)S(1)} %get-tuple-element.66), channel_id=1, source_target_pairs={{0,4},{2,6},{4,8},{6,10},{8,12},{10,14},{1,5},{3,7},{5,9},{7,11},{... | collective-permute-start | bytes 1572872 | tf_op jit(solution)/shard_map/ppermute | solution.py:52
  218.8 22.1 %collective-permute-start.24 = (bf16[512,512]{1,0:T(8,128)(2,1)S(1)}, bf16[512,512]{1,0:T(8,128)(2,1)S(1)}, u32[]{:S(2)}, u32[]{:S(2)}) collective-permute-start(bf16[512,512]{1,0:T(8,128)(2,1)S(1)} %get-tuple-element.69), channel_id=1, source_target_pairs={{0,4},{2,6},{4,8},{6,10},{8,12},{10,14},{1,5},{3,7},{5,9},{7,11},{... | collective-permute-start | bytes 1572872 | tf_op jit(solution)/shard_map/ppermute | solution.py:52
  223.0 18.0 %collective-permute-start.26 = (bf16[512,512]{1,0:T(8,128)(2,1)S(1)}, bf16[512,512]{1,0:T(8,128)(2,1)S(1)}, u32[]{:S(2)}, u32[]{:S(2)}) collective-permute-start(bf16[512,512]{1,0:T(8,128)(2,1)S(1)} %get-tuple-element.68), channel_id=1, source_target_pairs={{4,0},{6,2},{8,4},{10,6},{12,8},{14,10},{5,1},{7,3},{9,5},{11,7},{... | collective-permute-start | bytes 1572872 | tf_op jit(solution)/shard_map/ppermute | solution.py:52
  230.0 12.2 %collective-permute-start.36 = (bf16[256,512]{1,0:T(8,128)(2,1)S(1)}, bf16[256,512]{1,0:T(8,128)(2,1)S(1)}, u32[]{:S(2)}, u32[]{:S(2)}) collective-permute-start(bf16[256,512]{1,0:T(8,128)(2,1)S(1)} %constant_dynamic-slice_fusion), channel_id=1, source_target_pairs={{0,2},{2,0},{4,6},{6,4},{8,10},{10,8},{12,14},{14,12},{1,3},{3,1},... | collective-permute-start | bytes 786440 | tf_op jit(solution)/shard_map/ppermute | solution.py:34
  (16 other events, 131.0 us)

commit v2 on v1

--- a/solution.py
+++ b/solution.py
@@ -52,18 +52,27 @@
     return lax.ppermute(value, axis, pairs)
 
 
-def gather_line(block, axis, gates):
+def to_neighbours(value, axis):
+    groups = lax.axis_size(axis) // 2
+    return (
+        send_line(value, axis, upward=range(groups - 1)),
+        send_line(value, axis, downward=range(1, groups)),
+    )
+
+
+def gather_line(block, axis, gates, neighbours):
     groups, group = lax.axis_size(axis) // 2, lax.axis_index(axis) >> 1
-    out, up, down, either = [(group, block)], block, block, None
+    (up, down), out, either = neighbours, [(group, block)], None
     for hop in range(1, groups):
         upward, downward = range(hop - 1, groups - 1), range(1, groups - hop + 1)
         gate = gates.get(hop, ())
         below, above = jnp.maximum(group - hop, 0), jnp.minimum(group + hop, groups - 1)
         if either is None:
-            if gate:
-                up, down = after(up, *gate), after(down, *gate)
-            up = send_line(up, axis, upward=upward)
-            down = send_line(down, axis, downward=downward)
+            if hop > 1:
+                if gate:
+                    up, down = after(up, *gate), after(down, *gate)
+                up = send_line(up, axis, upward=upward)
+                down = send_line(down, axis, downward=downward)
             if 2 * hop < groups:
                 out += [(below, up), (above, down)]
                 continue
@@ -135,6 +144,39 @@
         ),
         name="split_tokens",
     )(tokens)
+
+
+def turn_kernel(place, mine, other, out):
+    length = mine.shape[0]
+    out[:length, :] = mine[...]
+    out[length:, :] = other[...]
+
+
+def turn(mine, other, place, blocks):
+    length, width = mine.shape
+    step = width // blocks
+    columns = pl.BlockSpec((length, step), lambda i, place: (0, i ^ place[0]))
+    if step % 128:
+        both = jnp.concatenate([mine, other], 0)
+        pieces = [
+            lax.dynamic_slice_in_dim(both, (i ^ place) * step, step, 1) for i in range(blocks)
+        ]
+        return jnp.concatenate(pieces, 1)
+    return pl.pallas_call(
+        turn_kernel,
+        grid_spec=pltpu.PrefetchScalarGridSpec(
+            num_scalar_prefetch=1,
+            grid=(blocks,),
+            in_specs=[columns, columns],
+            out_specs=pl.BlockSpec((2 * length, step), lambda i, place: (0, i)),
+        ),
+        out_shape=jax.ShapeDtypeStruct((2 * length, width), mine.dtype),
+        compiler_params=pltpu.CompilerParams(vmem_limit_bytes=16 * 1024 * 1024),
+        cost_estimate=pl.CostEstimate(
+            flops=0, bytes_accessed=12 * length * width, transcendentals=0
+        ),
+        name="turn_tokens",
+    )(place.reshape(1).astype(jnp.int32), mine, other)
 
 
 def attention_kernel(teacher_scale, student_scale, grad_scale, heads, *refs):
@@ -205,20 +247,20 @@
         grad_second[:, s_cols] = own[1]
 
 
-def attention(teacher, student, bias, live):
-    (length, width), ds = student[0].shape, DS // HEADS
+def attention(teacher, student, bias, live, chunk):
+    length, ds = student[0].shape[0], DS // HEADS
+    width = student[0].shape[1] // CHUNKS
     head_count = width // ds
-    dt = teacher[0].shape[1] // head_count
+    dt = teacher[0].shape[1] // CHUNKS // head_count
     heads = min(HEADS_A_STEP, head_count)
     student_scale = 1.0 / math.sqrt(ds)
     kernel = functools.partial(
         attention_kernel, 1.0 / math.sqrt(dt), student_scale, student_scale / HEADS, heads
     )
     steps = head_count // heads
-    inputs = lambda d: pl.BlockSpec((length, heads * d), lambda h: (0, h))
+    inputs = lambda d: pl.BlockSpec((length, heads * d), lambda h: (0, h + chunk * steps))
     columns = pl.BlockSpec((length, heads * ds), lambda h: (0, h))
     whole = lambda *shape: pl.BlockSpec(shape, lambda h: (0,) * len(shape))
-    flops = 2 * head_count * length * length * (4 * dt + 4 * ds + 8 * ds)
     return pl.pallas_call(
         kernel,
         grid=(steps,),
@@ -234,7 +276,7 @@
         ],
         compiler_params=pltpu.CompilerParams(vmem_limit_bytes=24 * 1024 * 1024),
         cost_estimate=pl.CostEstimate(
-            flops=flops,
+            flops=2 * head_count * length * length * (4 * dt + 12 * ds),
             bytes_accessed=6 * length * (dt + ds) * head_count + 8 * length * width,
             transcendentals=8 * length * length * head_count,
         ),
@@ -252,7 +294,6 @@
     piece_rows, my_width = block_rows // n_dp, width // 2
     chunk_width = my_width // CHUNKS
     teacher_width = teacher_part.shape[3] // n_tp
-    teacher_chunk = teacher_width // 2 // CHUNKS
     unscale = HEADS * math.sqrt(DS // HEADS)
     chunks = range(CHUNKS)
 
@@ -261,7 +302,10 @@
         return lax.dynamic_slice(out_proj, start, (piece_rows, my_width))
 
     kept, sent = weight_piece(place), weight_piece(1 - place)
+    own_rows = to_neighbours(kept, "ctx")
     swapped = swap(sent, "ctx", 1)
+    pair_rows = to_neighbours(after(swapped, *own_rows), "ctx")
+    neighbours = [jnp.concatenate(halves, 0) for halves in zip(own_rows, pair_rows)]
 
     pieces = split(after(tokens, kept, sent), n_ctx, n_dp)
 
@@ -272,61 +316,47 @@
     for steps in range(1, n_dp):
         documents.append(rotate(piece(lax.rem(my_dp + steps, n_dp)), "dp", steps))
     others = [swap(rows, "ctx", 1) for rows in documents]
-    pair = jnp.concatenate(ordered(kept, after(swapped, documents[-1]), place), 0)
-
-    def teacher_columns(owner, chunk):
-        starts = [
-            owner * teacher_width + (half * CHUNKS + chunk) * teacher_chunk for half in range(2)
-        ]
-        partial = after(teacher_part, kept, sent)[0, 0]
-        return [lax.dynamic_slice_in_dim(partial, start, teacher_chunk, 1) for start in starts]
-
-    kept_columns, left_columns = [], []
-    for chunk in chunks:
-        total = [part.astype(jnp.float32) for part in teacher_columns(my_tp, chunk)]
-        for steps in range(1, n_tp):
-            leaving = jnp.concatenate(teacher_columns(lax.rem(my_tp + steps, n_tp), chunk), 1)
-            arrived = rotate(after(leaving, pair) if chunk else leaving, "tp", steps)
-            if chunk:
-                arrived = after(arrived, kept_columns[-1], left_columns[-1])
-            total = [
-                t + arrived[:, half * teacher_chunk : (half + 1) * teacher_chunk].astype(jnp.float32)
-                for half, t in enumerate(total)
-            ]
-        mine, other = ordered(*[t.astype(jnp.bfloat16) for t in total], place)
-        kept_columns.append(mine)
-        left_columns.append(other)
-
-    teacher, turned = [], []
-    for mine, other in zip(kept_columns, left_columns):
-        if turned:
-            other = after(other, turned[-1])
-        turned.append(swap(other, "ctx", 1))
-        teacher.append(ordered(mine, turned[-1], place))
-
-    gates = {
-        2: (others[0], left_columns[0]),
-        groups - 1: (*others, left_columns[-1], turned[0]),
-    }
-    weights = gather_line(pair, "ctx", gates)
-    rows = [jnp.concatenate(pair_of, 0) for pair_of in zip(documents, others)]
+
+    def teacher_columns(owner):
+        return lax.dynamic_slice_in_dim(
+            after(teacher_part, kept, sent)[0, 0], owner * teacher_width, teacher_width, 1
+        )
+
+    total = teacher_columns(my_tp).astype(jnp.float32)
+    for steps in range(1, n_tp):
+        received = rotate(teacher_columns(lax.rem(my_tp + steps, n_tp)), "tp", steps)
+        total = total + received.astype(jnp.float32)
+    total = total.astype(jnp.bfloat16)
+    mine = lax.dynamic_slice_in_dim(total, place * (teacher_width // 2), teacher_width // 2, 1)
+    other = lax.dynamic_slice_in_dim(
+        total, (1 - place) * (teacher_width // 2), teacher_width // 2, 1
+    )
+    turned = swap(after(other, others[-1]), "ctx", 1)
+    teacher = ordered(mine, turned, place)
+    teacher = (shift(teacher[1], "ctx", 2), *teacher)
+
+    gates = {groups - 1: (others[0], other)}
+    weights = gather_line(jnp.concatenate([kept, swapped], 0), "ctx", gates, neighbours)
+    rows = [turn(mine, other, place, n_ctx) for mine, other in zip(documents, others)]
     rows_turned = row_major(jnp.concatenate(rows, 0).T)
-    weights[-1] = (weights[-1][0], after(weights[-1][1], rows_turned, turned[-1]))
-
-    def project(document):
-        product = 0.0
-        for source, block in weights:
-            inputs = lax.dynamic_slice_in_dim(
-                rows[document], source * (2 * piece_rows), 2 * piece_rows, 1
-            )
-            product = product + jnp.dot(inputs, block, preferred_element_type=jnp.float32)
-        return product
-
+
+    def product_of(document, source, block):
+        inputs = lax.dynamic_slice_in_dim(
+            rows[document], source * (2 * piece_rows), 2 * piece_rows, 1
+        )
+        return jnp.dot(inputs, block, preferred_element_type=jnp.float32)
+
+    early = [
+        sum(product_of(document, *weight) for weight in weights[:-1]) for document in range(n_dp)
+    ]
+    source, block = weights[-1]
+    block = after(block, *early, teacher[1], rows_turned)
     total = 0.0
     for steps in range(1, n_dp):
-        total = total + rotate(project(steps), "dp", -steps)
-    total = (project(0) + total).astype(jnp.bfloat16)
+        total = total + rotate(early[steps] + product_of(steps, source, block), "dp", -steps)
+    total = (early[0] + product_of(0, source, block) + total).astype(jnp.bfloat16)
     student = ordered(total[:length], total[length:], place)
+    student = (shift(student[1], "ctx", 2), *student)
 
     valid = valid_count[0]
     padded = jnp.concatenate([jnp.full((length,), -1, jnp.int32), segment_ids[0]], 0)
@@ -345,18 +375,14 @@
 
     results = []
     for chunk in chunks:
-        columns = slice(chunk * chunk_width, (chunk + 1) * chunk_width)
-        states = [half[:, columns] for half in student]
-        leaving = teacher[chunk][1]
-        teacher_past = shift(after(leaving, total) if chunk else leaving, "ctx", 2)
-        states = (shift(after(states[1], teacher_past), "ctx", 2), *states)
-        if results:
+        if chunk:
             live = after(live, results[-1][0])
-        results.append(attention((teacher_past, *teacher[chunk]), states, bias, live))
+        results.append(attention(teacher, student, bias, live, chunk))
 
     parts, state_grad, beside = [], [], ()
     for _, grad_past, grad_first, grad_second in results:
-        from_next = shift(grad_past, "ctx", -2).astype(jnp.float32)
+        from_next = shift(grad_past, "ctx", -2)
+        from_next = from_next.astype(jnp.float32)
         grad_second = (grad_second + from_next).astype(jnp.bfloat16)
         mine, other = ordered(grad_first, grad_second, place)
         block = jnp.concatenate([mine, other], 0)
@@ -368,8 +394,7 @@
         state_grad.append(ordered(mine, swap(after(other, blocks[-1]), "ctx", 1), place))
 
         total = total.astype(jnp.bfloat16)
-        mine = lax.dynamic_slice_in_dim(total, place * piece_rows, piece_rows, 0)
-        other = lax.dynamic_slice_in_dim(total, (1 - place) * piece_rows, piece_rows, 0)
+        mine, other = total[:piece_rows], total[piece_rows:]
         total = jnp.concatenate(ordered(mine, swap(other, "ctx", 1), place), 1)
         owners = [total] + [rotate(total, "dp", steps) for steps in range(1, n_dp)]
         parts.append(jnp.concatenate(by_owner(owners, my_dp), 0))

time: 259 us -> 267 us (1.031)
  local copies, waits for them, and re-layouts: 11.7 us -> 21 us
  Pallas kernels: 12.4 us -> 18 us
  starting transfers between devices: 83.8 us -> 78.5 us
    ppermute x6 -> x4, waiting for transfers between devices: 8.34 us -> 26.8 us  [shift(): return lax.ppermute(value, axis, pairs)]
    ppermute x15 -> x17, waiting for transfers between devices: 55.6 us -> 40 us  [send_line(): return lax.ppermute(value, axis, pairs)]
    ppermute x6 -> x4, starting transfers between devices: 16.9 us -> 8.99 us  [shift(): return lax.ppermute(value, axis, pairs)]
    ppermute x15 -> x17, starting transfers between devices: 36.1 us -> 43 us  [send_line(): return lax.ppermute(value, axis, pairs)]
    unnamed x13 -> x42, local copies, waits for them, and re-layouts: 2.02 us -> 8.8 us
    select_n x3 -> x0, other arithmetic: 5.74 us -> none  [ordered(): second = lax.select(place == 0, other, mine)]
    pallas_call x0 -> x2, local copies, waits for them, and re-layouts: none -> 5.41 us  [turn(): pl.pallas_call(turn_kernel, grid_spec=pltpu.PrefetchScalarGridSpec(num_sc...]
    ppermute x13 -> x12, waiting for transfers between devices: 27.2 us -> 22 us  [swap(): return lax.ppermute(value, axis, [(i, i ^ distance) for i in range(count)])]
  transfers between devices with their start and end apart: 42 -> 40, of which waited for: 19 -> 21; matrix products, arithmetic and copies ran while one was open for 19% -> 20% of each run, Pallas kernels for 5% -> 4%
where the time goes in v2:
time: 267 us; the launch traced here: 265 us
  waiting for transfers between devices  97.1 us (36%)
  starting transfers between devices  78.5 us (29%)
  other arithmetic  27.9 us (10%)
  local copies, waits for them, and re-layouts  21 us (8%)
  matrix products  19.3 us (7%)
  Pallas kernels  18 us (7%)
  between operations  3.48 us (1%)
    ppermute x17, starting transfers between devices, send_line(): return lax.ppermute(value, axis, pairs)  43 us
    ppermute x17, waiting for transfers between devices, send_line(): return lax.ppermute(value, axis, pairs)  40 us
    ppermute x4, waiting for transfers between devices, shift(): return lax.ppermute(value, axis, pairs)  26.8 us
    ppermute x12, waiting for transfers between devices, swap(): return lax.ppermute(value, axis, [(i, i ^ distance) for i in range(count)])  22 us
    ppermute x7, starting transfers between devices, rotate(): lax.ppermute(value, axis, [(i, (i + steps) % count) for i in range(count)])  15.6 us
    dot_general x10, matrix products, product_of(): return jnp.dot(inputs, block, preferred_element_type=jnp.float32)  13.6 us
    pallas_call x2, Pallas kernels, attention(): pl.pallas_call(kernel, grid=(steps,), in_specs=[inputs(dt)] * 3 + [inputs...  12.5 us
    ppermute x12, starting transfers between devices, swap(): return lax.ppermute(value, axis, [(i, i ^ distance) for i in range(count)])  10.9 us
  transfers between devices with their start and end apart: 40, of which 21 were waited for; matrix products, arithmetic and copies ran while one was open for 20% of the time, Pallas kernels for 4%

profile of v2, /device:TPU:1, one launch (start us, length us, event | category | flops | bytes accessed | tf_op | source)
XLA Modules:
  0.0 265.2 jit_solution(10623109899060091062)
XLA Ops:
  2.9 4.8 %collective-permute-start.7 = (bf16[256,1024]{1,0:T(8,128)(2,1)}, bf16[256,1024]{1,0:T(8,128)(2,1)}, u32[]{:S(2)}, u32[]{:S(2)}) collective-permute-start(bf16[256,1024]{1,0:T(8,128)(2,1)} %get-tuple-element.56), channel_id=1, source_target_pairs={{0,4},{2,6},{4,8},{6,10},{8,12},{10,14},{1,5},{3,7},{5,9},{7,11},{... | collective-permute-start | bytes 1572872 | tf_op jit(solution)/shard_map/ppermute | solution.py:52
  10.3 3.1 %dynamic-slice_bitcast_fusion = bf16[256,4096]{1,0:T(8,128)(2,1)} fusion(bf16[1,1,256,8192]{3,2,1,0:T(8,128)(2,1)} %param.5, s32[]{:T(128)S(6)} %select_n.232), kind=kLoop, calls=%fused_computation.20 | loop fusion | bytes 4194308 | tf_op jit(solution)/shard_map/dynamic_slice | solution.py:321
  22.4 3.2 %collective-permute-start.9 = (bf16[256,1024]{1,0:T(8,128)(2,1)}, bf16[256,1024]{1,0:T(8,128)(2,1)S(1)}, u32[]{:S(2)}, u32[]{:S(2)}) collective-permute-start(bf16[256,1024]{1,0:T(8,128)(2,1)} %collective-permute-done.6), channel_id=1, source_target_pairs={{0,4},{2,6},{4,8},{6,10},{8,12},{10,14},{1,5},{3,7},{5,9},{7,11},{... | collective-permute-start | bytes 1572872 | tf_op jit(solution)/shard_map/ppermute | solution.py:52
  29.1 5.1 %collective-permute-done.9 = bf16[256,1024]{1,0:T(8,128)(2,1)S(1)} collective-permute-done((bf16[256,1024]{1,0:T(8,128)(2,1)}, bf16[256,1024]{1,0:T(8,128)(2,1)S(1)}, u32[]{:S(2)}, u32[]{:S(2)}) %collective-permute-start.9) | collective-permute-done | bytes 524320 | tf_op jit(solution)/shard_map/ppermute | solution.py:52
  35.0 3.1 %collective-permute-done.10 = bf16[256,1024]{1,0:T(8,128)(2,1)S(1)} collective-permute-done((bf16[256,1024]{1,0:T(8,128)(2,1)}, bf16[256,1024]{1,0:T(8,128)(2,1)S(1)}, u32[]{:S(2)}, u32[]{:S(2)}) %collective-permute-start.10) | collective-permute-done | bytes 524320 | tf_op jit(solution)/shard_map/ppermute | solution.py:52
  39.8 5.1 %collective-permute-done.5.other = bf16[256,2048]{1,0:T(8,128)(2,1)S(1)} collective-permute-done((bf16[256,2048]{1,0:T(8,128)(2,1)S(1)}, bf16[256,2048]{1,0:T(8,128)(2,1)S(1)}, u32[]{:S(2)}, u32[]{:S(2)}) %collective-permute-start.5) | collective-permute-done | bytes 1048608 | tf_op jit(solution)/shard_map/ppermute | solution.py:34
  51.3 8.3 %collective-permute-done = bf16[256,4096]{1,0:T(8,128)(2,1)} collective-permute-done((bf16[256,4096]{1,0:T(8,128)(2,1)}, bf16[256,4096]{1,0:T(8,128)(2,1)}, u32[]{:S(2)}, u32[]{:S(2)}) %collective-permute-start) | collective-permute-done | bytes 2097184 | tf_op jit(solution)/shard_map/ppermute | solution.py:29
  62.1 4.8 %collective-permute-done.2.other = bf16[256,2048]{1,0:T(8,128)(2,1)S(1)} collective-permute-done((bf16[256,2048]{1,0:T(8,128)(2,1)}, bf16[256,2048]{1,0:T(8,128)(2,1)S(1)}, u32[]{:S(2)}, u32[]{:S(2)}) %collective-permute-start.2) | collective-permute-done | bytes 1048608 | tf_op jit(solution)/shard_map/ppermute | solution.py:34
  67.9 4.0 %turn_tokens.3 = bf16[512,2048]{1,0:T(8,128)(2,1)S(1)} custom-call(s32[1]{0:T(128)} %bitcast.4.place, bf16[256,2048]{1,0:T(8,128)(2,1)} %collective-permute-done.1.mine, bf16[256,2048]{1,0:T(8,128)(2,1)S(1)} %collective-permute-done.2.other), custom_call_target="tpu_custom_call" | custom-call | bytes 6291456 | tf_op jit(solution)/shard_map/turn_tokens/pallas_call | solution.py:165
  79.7 10.4 %collective-permute-done.3 = bf16[256,2048]{1,0:T(8,128)(2,1)S(1)} collective-permute-done((bf16[256,2048]{1,0:T(8,128)(2,1)S(1)}, bf16[256,2048]{1,0:T(8,128)(2,1)S(1)}, u32[]{:S(2)}, u32[]{:S(2)}) %collective-permute-start.3) | collective-permute-done | bytes 1048608 | tf_op jit(solution)/shard_map/ppermute | solution.py:34
  91.5 7.2 %collective-permute-done.13 = bf16[512,1024]{1,0:T(8,128)(2,1)S(1)} collective-permute-done((bf16[512,1024]{1,0:T(8,128)(2,1)S(1)}, bf16[512,1024]{1,0:T(8,128)(2,1)S(1)}, u32[]{:S(2)}, u32[]{:S(2)}) %collective-permute-start.13) | collective-permute-done | bytes 1048608 | tf_op jit(solution)/shard_map/ppermute | solution.py:52
  100.7 3.1 %collective-permute-start.14 = (f32[512,1024]{1,0:T(8,128)}, f32[512,1024]{1,0:T(8,128)}, u32[]{:S(2)}, u32[]{:S(2)}) collective-permute-start(f32[512,1024]{1,0:T(8,128)} %convolution_add_fusion), channel_id=1, source_target_pairs={{0,16},{16,0},{1,17},{17,1},{2,18},{18,2},{3,19},{19,3},{4,20},{20... | collective-permute-start | bytes 6291464 | tf_op jit(solution)/shard_map/ppermute | solution.py:29
  110.3 5.1 %collective-permute-start.15 = (bf16[256,1024]{1,0:T(8,128)(2,1)S(1)}, bf16[256,1024]{1,0:T(8,128)(2,1)S(1)}, u32[]{:S(2)}, u32[]{:S(2)}) collective-permute-start(bf16[256,1024]{1,0:T(8,128)(2,1)S(1)} %get-tuple-element.66.refs_5_), channel_id=1, source_target_pairs={{0,4},{2,6},{4,8},{6,10},{8,12},{10,14},{1,5},{3,7},{5,9},{7,11},{... | collective-permute-start | bytes 1572872 | tf_op jit(solution)/shard_map/ppermute | solution.py:40
  115.7 13.2 %collective-permute-done.4.refs_0_ = bf16[256,2048]{1,0:T(8,128)(2,1)S(1)} collective-permute-done((bf16[256,2048]{1,0:T(8,128)(2,1)}, bf16[256,2048]{1,0:T(8,128)(2,1)S(1)}, u32[]{:S(2)}, u32[]{:S(2)}) %collective-permute-start.4) | collective-permute-done | bytes 1048608 | tf_op jit(solution)/shard_map/ppermute | solution.py:40
  128.9 11.1 %collective-permute-done.15.refs_3_ = bf16[256,1024]{1,0:T(8,128)(2,1)S(1)} collective-permute-done((bf16[256,1024]{1,0:T(8,128)(2,1)S(1)}, bf16[256,1024]{1,0:T(8,128)(2,1)S(1)}, u32[]{:S(2)}, u32[]{:S(2)}) %collective-permute-start.15) | collective-permute-done | bytes 524320 | tf_op jit(solution)/shard_map/ppermute | solution.py:40
  140.0 6.1 %window_attention.2 = (f32[1,256]{1,0:T(1,128)S(1)}, bf16[256,512]{1,0:T(8,128)(2,1)S(1)}, bf16[256,512]{1,0:T(8,128)(2,1)S(1)}, f32[256,512]{1,0:T(8,128)S(1)}) custom-call(bf16[256,2048]{1,0:T(8,128)(2,1)S(1)} %collective-permute-done.4.refs_0_, bf16[256,2048]{1,0:T(8,128)(2,1)S(1)} %get-tuple-element.51.refs_1_, bf16[256,2048]{1,0:T(8,128)(2,1)S(1)} %copy-done.1, ...), custom_call_target="tpu_custom_call" | custom-call | flops 1342177280 | bytes 3407872 | tf_op jit(solution)/shard_map/window_attention/pallas_call | solution.py:264
  147.4 6.5 %window_attention.3 = (f32[1,256]{1,0:T(1,128)S(1)}, bf16[256,512]{1,0:T(8,128)(2,1)}, bf16[256,512]{1,0:T(8,128)(2,1)S(1)}, f32[256,512]{1,0:T(8,128)S(1)}) custom-call(bf16[256,2048]{1,0:T(8,128)(2,1)S(1)} %collective-permute-done.4.refs_0_, bf16[256,2048]{1,0:T(8,128)(2,1)S(1)} %get-tuple-element.51.refs_1_, bf16[256,2048]{1,0:T(8,128)(2,1)S(1)} %copy-done.1, ...), custom_call_target="tpu_custom_call" | custom-call | flops 1342177280 | bytes 3407872 | tf_op jit(solution)/shard_map/window_attention/pallas_call | solution.py:264
  161.7 2.9 %copy.9 = bf16[512,2048]{0,1:T(8,128)(2,1)S(1)} copy(bf16[512,2048]{1,0:T(8,128)(2,1)} %copy-done) | data formatting | bytes 4194304 | tf_op jit(solution)/shard_map/turn_tokens/pallas_call | solution.py:165
  168.9 3.4 %fusion.17 = f32[2048,512]{1,0:T(8,128)S(1)} fusion(bf16[512,512]{1,0:T(8,128)(2,1)} %collective-permute-done.28, bf16[256,512]{1,0:T(8,128)(2,1)S(1)} %copy-done.15, bf16[256,512]{1,0:T(8,128)(2,1)S(1)} %get-tuple-element.59, bf16[512,2048]{0,1:T(8,128)(2,1)S(1)} %copy.9, bf16[512,2048]{0,1:T(8,128)(2,1)S(1)} %copy-done.13), kind=kOutput, calls=%fused_computation.29 | convolution fusion | flops 2159017984 | bytes 9437184 | tf_op jit(solution)/shard_map/dot_general | solution.py:390
  172.4 5.0 %collective-permute-start.29 = (bf16[512,512]{1,0:T(8,128)(2,1)S(1)}, bf16[512,512]{1,0:T(8,128)(2,1)}, u32[]{:S(2)}, u32[]{:S(2)}) collective-permute-start(bf16[512,512]{1,0:T(8,128)(2,1)S(1)} %fusion.39), channel_id=1, source_target_pairs={{0,4},{2,6},{12,8},{14,10},{1,5},{3,7},{13,9},{15,11},{16,20},{18,... | collective-permute-start | bytes 1572872 | tf_op jit(solution)/shard_map/ppermute | solution.py:52
  187.8 2.8 %fusion.27 = (bf16[512,512]{1,0:T(8,128)(2,1)}, bf16[512,512]{1,0:T(8,128)(2,1)S(1)}) fusion(f32[4,512,512]{2,1,0:T(8,128)} %bitcast.93, s32[]{:T(128)S(6)} %select_n.260, bf16[512,512]{1,0:T(8,128)(2,1)} %collective-permute-done.29, pred[]{:T(512)S(6)} %le.4, pred[]{:T(512)S(6)} %ge.4, s32[]{:T(128)S(6)} %max.7), kind=kLoop, calls=%fused_computation.47 | loop fusion | flops 2097152 | bytes 3670026 | tf_op jit(solution)/shard_map/convert_element_type | solution.py:98
  190.6 4.4 %collective-permute-start.30 = (bf16[512,512]{1,0:T(8,128)(2,1)}, bf16[512,512]{1,0:T(8,128)(2,1)S(1)}, u32[]{:S(2)}, u32[]{:S(2)}) collective-permute-start(bf16[512,512]{1,0:T(8,128)(2,1)} %get-tuple-element.43), channel_id=1, source_target_pairs={{0,4},{2,6},{4,8},{6,10},{1,5},{3,7},{5,9},{7,11},{16,20},{18,22},... | collective-permute-start | bytes 1572872 | tf_op jit(solution)/shard_map/ppermute | solution.py:52
  201.7 4.1 %collective-permute-start.21 = (bf16[512,512]{1,0:T(8,128)(2,1)}, bf16[512,512]{1,0:T(8,128)(2,1)S(1)}, u32[]{:S(2)}, u32[]{:S(2)}) collective-permute-start(bf16[512,512]{1,0:T(8,128)(2,1)} %get-tuple-element.46), channel_id=1, source_target_pairs={{0,4},{2,6},{4,8},{6,10},{1,5},{3,7},{5,9},{7,11},{16,20},{18,22},... | collective-permute-start | bytes 1572872 | tf_op jit(solution)/shard_map/ppermute | solution.py:52
  213.6 4.1 %collective-permute-start.31 = (bf16[512,512]{1,0:T(8,128)(2,1)S(1)}, bf16[512,512]{1,0:T(8,128)(2,1)S(1)}, u32[]{:S(2)}, u32[]{:S(2)}) collective-permute-start(bf16[512,512]{1,0:T(8,128)(2,1)S(1)} %get-tuple-element.47), channel_id=1, source_target_pairs={{0,4},{2,6},{4,8},{6,10},{8,12},{10,14},{1,5},{3,7},{5,9},{7,11},{... | collective-permute-start | bytes 1572872 | tf_op jit(solution)/shard_map/ppermute | solution.py:52
  217.8 3.8 %collective-permute-done.21 = bf16[512,512]{1,0:T(8,128)(2,1)S(1)} collective-permute-done((bf16[512,512]{1,0:T(8,128)(2,1)}, bf16[512,512]{1,0:T(8,128)(2,1)S(1)}, u32[]{:S(2)}, u32[]{:S(2)}) %collective-permute-start.21) | collective-permute-done | bytes 524320 | tf_op jit(solution)/shard_map/ppermute | solution.py:52
  224.4 4.7 %collective-permute-start.22 = (bf16[512,512]{1,0:T(8,128)(2,1)S(1)}, bf16[512,512]{1,0:T(8,128)(2,1)S(1)}, u32[]{:S(2)}, u32[]{:S(2)}) collective-permute-start(bf16[512,512]{1,0:T(8,128)(2,1)S(1)} %get-tuple-element.50), channel_id=1, source_target_pairs={{0,4},{2,6},{4,8},{6,10},{8,12},{10,14},{1,5},{3,7},{5,9},{7,11},{... | collective-permute-start | bytes 1572872 | tf_op jit(solution)/shard_map/ppermute | solution.py:52
  232.7 3.9 %collective-permute-done.33 = bf16[512,512]{1,0:T(8,128)(2,1)S(1)} collective-permute-done((bf16[512,512]{1,0:T(8,128)(2,1)S(1)}, bf16[512,512]{1,0:T(8,128)(2,1)S(1)}, u32[]{:S(2)}, u32[]{:S(2)}) %collective-permute-start.33) | collective-permute-done | bytes 524320 | tf_op jit(solution)/shard_map/ppermute | solution.py:52
  239.4 4.5 %collective-permute-done.22 = bf16[512,512]{1,0:T(8,128)(2,1)S(1)} collective-permute-done((bf16[512,512]{1,0:T(8,128)(2,1)S(1)}, bf16[512,512]{1,0:T(8,128)(2,1)S(1)}, u32[]{:S(2)}, u32[]{:S(2)}) %collective-permute-start.22) | collective-permute-done | bytes 524320 | tf_op jit(solution)/shard_map/ppermute | solution.py:52
  244.0 3.9 %collective-permute-done.24 = bf16[512,512]{1,0:T(8,128)(2,1)S(1)} collective-permute-done((bf16[512,512]{1,0:T(8,128)(2,1)S(1)}, bf16[512,512]{1,0:T(8,128)(2,1)S(1)}, u32[]{:S(2)}, u32[]{:S(2)}) %collective-permute-start.24) | collective-permute-done | bytes 524320 | tf_op jit(solution)/shard_map/ppermute | solution.py:52
  250.8 3.4 %collective-permute-start.35 = (bf16[256,1024]{1,0:T(8,128)(2,1)S(1)}, bf16[256,1024]{1,0:T(8,128)(2,1)S(1)}, u32[]{:S(2)}, u32[]{:S(2)}) collective-permute-start(bf16[256,1024]{1,0:T(8,128)(2,1)S(1)} %pad_maximum_fusion.5), channel_id=1, source_target_pairs={{0,16},{16,0},{1,17},{17,1},{2,18},{18,2},{3,19},{19,3},{4,20},{20... | collective-permute-start | bytes 1572872 | tf_op jit(solution)/shard_map/ppermute | solution.py:29
  254.7 3.7 %collective-permute-start.37 = (bf16[256,1024]{1,0:T(8,128)(2,1)S(1)}, bf16[256,1024]{1,0:T(8,128)(2,1)S(1)}, u32[]{:S(2)}, u32[]{:S(2)}) collective-permute-start(bf16[256,1024]{1,0:T(8,128)(2,1)S(1)} %pad_maximum_fusion.6), channel_id=1, source_target_pairs={{0,16},{16,0},{1,17},{17,1},{2,18},{18,2},{3,19},{19,3},{4,20},{20... | collective-permute-start | bytes 1572872 | tf_op jit(solution)/shard_map/ppermute | solution.py:29
  261.0 4.2 %fusion.9 = f32[512,2048]{1,0:T(8,128)} fusion(bf16[256,1024]{1,0:T(8,128)(2,1)S(1)} %get-tuple-element.62, bf16[256,1024]{1,0:T(8,128)(2,1)S(1)} %get-tuple-element.61, bf16[256,1024]{1,0:T(8,128)(2,1)S(1)} %get-tuple-element.58, bf16[256,1024]{1,0:T(8,128)(2,1)S(1)} %get-tuple-element.57, bf16[512,512]{1,0:T(8,128)(2,1)S(1)} %fusion.40, ...), kind=kLoop, calls=%fused_computation.14 | loop fusion | flops 20971520 | bytes 7340032 | tf_op jit(solution)/shard_map/convert_element_type | solution.py:415
  (160 shorter events, 98.9 us)
Async XLA Ops:
  2.9 16.7 %collective-permute-start.7 = (bf16[256,1024]{1,0:T(8,128)(2,1)}, bf16[256,1024]{1,0:T(8,128)(2,1)}, u32[]{:S(2)}, u32[]{:S(2)}) collective-permute-start(bf16[256,1024]{1,0:T(8,128)(2,1)} %get-tuple-element.56), channel_id=1, source_target_pairs={{0,4},{2,6},{4,8},{6,10},{8,12},{10,14},{1,5},{3,7},{5,9},{7,11},{... | collective-permute-start | bytes 1572872 | tf_op jit(solution)/shard_map/ppermute | solution.py:52
  7.7 14.7 %collective-permute-start.8 = (bf16[256,1024]{1,0:T(8,128)(2,1)}, bf16[256,1024]{1,0:T(8,128)(2,1)}, u32[]{:S(2)}, u32[]{:S(2)}) collective-permute-start(bf16[256,1024]{1,0:T(8,128)(2,1)} %get-tuple-element.56), channel_id=1, source_target_pairs={{4,0},{6,2},{8,4},{10,6},{12,8},{14,10},{5,1},{7,3},{9,5},{11,7},{... | collective-permute-start | bytes 1572872 | tf_op jit(solution)/shard_map/ppermute | solution.py:52
  9.0 13.4 %collective-permute-start.6 = (bf16[256,1024]{1,0:T(8,128)(2,1)}, bf16[256,1024]{1,0:T(8,128)(2,1)}, u32[]{:S(2)}, u32[]{:S(2)}) collective-permute-start(bf16[256,1024]{1,0:T(8,128)(2,1)} %get-tuple-element.55), channel_id=1, source_target_pairs={{0,2},{2,0},{4,6},{6,4},{8,10},{10,8},{12,14},{14,12},{1,3},{3,1},... | collective-permute-start | bytes 1572872 | tf_op jit(solution)/shard_map/ppermute | solution.py:34
  13.4 46.2 %collective-permute-start = (bf16[256,4096]{1,0:T(8,128)(2,1)}, bf16[256,4096]{1,0:T(8,128)(2,1)}, u32[]{:S(2)}, u32[]{:S(2)}) collective-permute-start(bf16[256,4096]{1,0:T(8,128)(2,1)} %dynamic-slice_bitcast_fusion), channel_id=1, source_target_pairs={{0,1},{1,0},{2,3},{3,2},{4,5},{5,4},{6,7},{7,6},{8,9},{9,8},{10,11... | collective-permute-start | bytes 6291464 | tf_op jit(solution)/shard_map/ppermute | solution.py:29
  18.0 21.4 %collective-permute-start.1 = (bf16[256,2048]{1,0:T(8,128)(2,1)}, bf16[256,2048]{1,0:T(8,128)(2,1)}, u32[]{:S(2)}, u32[]{:S(2)}) collective-permute-start(bf16[256,2048]{1,0:T(8,128)(2,1)} %get-tuple-element.54), channel_id=1, source_target_pairs={{0,16},{16,0},{1,17},{17,1},{2,18},{18,2},{3,19},{19,3},{4,20},{20... | collective-permute-start | bytes 3145736 | tf_op jit(solution)/shard_map/ppermute | solution.py:29
  19.5 25.3 %collective-permute-start.5 = (bf16[256,2048]{1,0:T(8,128)(2,1)S(1)}, bf16[256,2048]{1,0:T(8,128)(2,1)S(1)}, u32[]{:S(2)}, u32[]{:S(2)}) collective-permute-start(bf16[256,2048]{1,0:T(8,128)(2,1)S(1)} %get-tuple-element.53.mine), channel_id=1, source_target_pairs={{0,2},{2,0},{4,6},{6,4},{8,10},{10,8},{12,14},{14,12},{1,3},{3,1},... | collective-permute-start | bytes 3145736 | tf_op jit(solution)/shard_map/ppermute | solution.py:34
  22.4 11.8 %collective-permute-start.9 = (bf16[256,1024]{1,0:T(8,128)(2,1)}, bf16[256,1024]{1,0:T(8,128)(2,1)S(1)}, u32[]{:S(2)}, u32[]{:S(2)}) collective-permute-start(bf16[256,1024]{1,0:T(8,128)(2,1)} %collective-permute-done.6), channel_id=1, source_target_pairs={{0,4},{2,6},{4,8},{6,10},{8,12},{10,14},{1,5},{3,7},{5,9},{7,11},{... | collective-permute-start | bytes 1572872 | tf_op jit(solution)/shard_map/ppermute | solution.py:52
  25.6 12.5 %collective-permute-start.10 = (bf16[256,1024]{1,0:T(8,128)(2,1)}, bf16[256,1024]{1,0:T(8,128)(2,1)S(1)}, u32[]{:S(2)}, u32[]{:S(2)}) collective-permute-start(bf16[256,1024]{1,0:T(8,128)(2,1)} %collective-permute-done.6), channel_id=1, source_target_pairs={{4,0},{6,2},{8,4},{10,6},{12,8},{14,10},{5,1},{7,3},{9,5},{11,7},{... | collective-permute-start | bytes 1572872 | tf_op jit(solution)/shard_map/ppermute | solution.py:52
  34.3 39.1 %collective-permute-start.11 = (bf16[512,1024]{1,0:T(8,128)(2,1)S(1)}, bf16[512,1024]{1,0:T(8,128)(2,1)S(1)}, u32[]{:S(2)}, u32[]{:S(2)}) collective-permute-start(bf16[512,1024]{1,0:T(8,128)(2,1)S(1)} %constant_dynamic-update-slice_fusion), channel_id=1, source_target_pairs={{4,8},{6,10},{8,12},{10,14},{5,9},{7,11},{9,13},{11,15},{20,24},{2... | collective-permute-start | bytes 3145736 | tf_op jit(solution)/shard_map/ppermute | solution.py:52
  38.1 35.3 %collective-permute-start.12 = (bf16[512,1024]{1,0:T(8,128)(2,1)S(1)}, bf16[512,1024]{1,0:T(8,128)(2,1)S(1)}, u32[]{:S(2)}, u32[]{:S(2)}) collective-permute-start(bf16[512,1024]{1,0:T(8,128)(2,1)S(1)} %constant_dynamic-update-slice_fusion.2), channel_id=1, source_target_pairs={{4,0},{6,2},{8,4},{10,6},{5,1},{7,3},{9,5},{11,7},{20,16},{22,18},... | collective-permute-start | bytes 3145736 | tf_op jit(solution)/shard_map/ppermute | solution.py:52
  39.4 27.5 %collective-permute-start.2 = (bf16[256,2048]{1,0:T(8,128)(2,1)}, bf16[256,2048]{1,0:T(8,128)(2,1)S(1)}, u32[]{:S(2)}, u32[]{:S(2)}) collective-permute-start(bf16[256,2048]{1,0:T(8,128)(2,1)} %collective-permute-done.1.mine), channel_id=1, source_target_pairs={{0,2},{2,0},{4,6},{6,4},{8,10},{10,8},{12,14},{14,12},{1,3},{3,1},... | collective-permute-start | bytes 3145736 | tf_op jit(solution)/shard_map/ppermute | solution.py:34
  67.0 23.1 %collective-permute-start.3 = (bf16[256,2048]{1,0:T(8,128)(2,1)S(1)}, bf16[256,2048]{1,0:T(8,128)(2,1)S(1)}, u32[]{:S(2)}, u32[]{:S(2)}) collective-permute-start(bf16[256,2048]{1,0:T(8,128)(2,1)S(1)} %constant_dynamic-slice_fusion), channel_id=1, source_target_pairs={{0,2},{2,0},{4,6},{6,4},{8,10},{10,8},{12,14},{14,12},{1,3},{3,1},... | collective-permute-start | bytes 3145736 | tf_op jit(solution)/shard_map/ppermute | solution.py:34
  74.2 24.4 %collective-permute-start.13 = (bf16[512,1024]{1,0:T(8,128)(2,1)S(1)}, bf16[512,1024]{1,0:T(8,128)(2,1)S(1)}, u32[]{:S(2)}, u32[]{:S(2)}) collective-permute-start(bf16[512,1024]{1,0:T(8,128)(2,1)S(1)} %broadcast_select_fusion), channel_id=1, source_target_pairs={{8,12},{10,14},{4,0},{6,2},{9,13},{11,15},{5,1},{7,3},{24,28},{26,... | collective-permute-start | bytes 3145736 | tf_op jit(solution)/shard_map/ppermute | solution.py:52
  104.7 24.2 %collective-permute-start.4 = (bf16[256,2048]{1,0:T(8,128)(2,1)}, bf16[256,2048]{1,0:T(8,128)(2,1)S(1)}, u32[]{:S(2)}, u32[]{:S(2)}) collective-permute-start(bf16[256,2048]{1,0:T(8,128)(2,1)} %get-tuple-element.52.refs_2_), channel_id=1, source_target_pairs={{0,4},{2,6},{4,8},{6,10},{8,12},{10,14},{1,5},{3,7},{5,9},{7,11},{... | collective-permute-start | bytes 3145736 | tf_op jit(solution)/shard_map/ppermute | solution.py:40
  110.3 29.7 %collective-permute-start.15 = (bf16[256,1024]{1,0:T(8,128)(2,1)S(1)}, bf16[256,1024]{1,0:T(8,128)(2,1)S(1)}, u32[]{:S(2)}, u32[]{:S(2)}) collective-permute-start(bf16[256,1024]{1,0:T(8,128)(2,1)S(1)} %get-tuple-element.66.refs_5_), channel_id=1, source_target_pairs={{0,4},{2,6},{4,8},{6,10},{8,12},{10,14},{1,5},{3,7},{5,9},{7,11},{... | collective-permute-start | bytes 1572872 | tf_op jit(solution)/shard_map/ppermute | solution.py:40
  146.1 10.6 %collective-permute-start.27 = (bf16[256,512]{1,0:T(8,128)(2,1)S(1)}, bf16[256,512]{1,0:T(8,128)(2,1)S(1)}, u32[]{:S(2)}, u32[]{:S(2)}) collective-permute-start(bf16[256,512]{1,0:T(8,128)(2,1)S(1)} %get-tuple-element.38), channel_id=1, source_target_pairs={{4,0},{6,2},{8,4},{10,6},{12,8},{14,10},{5,1},{7,3},{9,5},{11,7},{... | collective-permute-start | bytes 786440 | tf_op jit(solution)/shard_map/ppermute | solution.py:40
  154.7 11.6 %collective-permute-start.18 = (bf16[256,512]{1,0:T(8,128)(2,1)}, bf16[256,512]{1,0:T(8,128)(2,1)}, u32[]{:S(2)}, u32[]{:S(2)}) collective-permute-start(bf16[256,512]{1,0:T(8,128)(2,1)} %get-tuple-element.33), channel_id=1, source_target_pairs={{4,0},{6,2},{8,4},{10,6},{12,8},{14,10},{5,1},{7,3},{9,5},{11,7},{... | collective-permute-start | bytes 786440 | tf_op jit(solution)/shard_map/ppermute | solution.py:40
  157.8 11.0 %collective-permute-start.28 = (bf16[512,512]{1,0:T(8,128)(2,1)}, bf16[512,512]{1,0:T(8,128)(2,1)}, u32[]{:S(2)}, u32[]{:S(2)}) collective-permute-start(bf16[512,512]{1,0:T(8,128)(2,1)} %pad_maximum_fusion.4), channel_id=1, source_target_pairs={{0,16},{16,0},{1,17},{17,1},{2,18},{18,2},{3,19},{19,3},{4,20},{20... | collective-permute-start | bytes 1572872 | tf_op jit(solution)/shard_map/ppermute | solution.py:29
  172.4 15.4 %collective-permute-start.29 = (bf16[512,512]{1,0:T(8,128)(2,1)S(1)}, bf16[512,512]{1,0:T(8,128)(2,1)}, u32[]{:S(2)}, u32[]{:S(2)}) collective-permute-start(bf16[512,512]{1,0:T(8,128)(2,1)S(1)} %fusion.39), channel_id=1, source_target_pairs={{0,4},{2,6},{12,8},{14,10},{1,5},{3,7},{13,9},{15,11},{16,20},{18,... | collective-permute-start | bytes 1572872 | tf_op jit(solution)/shard_map/ppermute | solution.py:52
  181.8 17.2 %collective-permute-start.20 = (bf16[512,512]{1,0:T(8,128)(2,1)S(1)}, bf16[512,512]{1,0:T(8,128)(2,1)S(1)}, u32[]{:S(2)}, u32[]{:S(2)}) collective-permute-start(bf16[512,512]{1,0:T(8,128)(2,1)S(1)} %fusion.37), channel_id=1, source_target_pairs={{0,4},{2,6},{12,8},{14,10},{1,5},{3,7},{13,9},{15,11},{16,20},{18,... | collective-permute-start | bytes 1572872 | tf_op jit(solution)/shard_map/ppermute | solution.py:52
  185.7 21.7 %collective-permute-start.16 = (f32[1,128]{1,0:T(1,128)S(1)}, f32[1,128]{1,0:T(1,128)S(1)}, u32[]{:S(2)}, u32[]{:S(2)}) collective-permute-start(f32[1,128]{1,0:T(1,128)S(1)} %broadcast_in_dim.34), channel_id=1, source_target_pairs={{0,1},{1,0},{2,3},{3,2},{4,5},{5,4},{6,7},{7,6},{8,9},{9,8},{10,11... | collective-permute-start | bytes 1544 | tf_op jit(solution)/shard_map/ppermute | solution.py:34
  190.6 20.5 %collective-permute-start.30 = (bf16[512,512]{1,0:T(8,128)(2,1)}, bf16[512,512]{1,0:T(8,128)(2,1)S(1)}, u32[]{:S(2)}, u32[]{:S(2)}) collective-permute-start(bf16[512,512]{1,0:T(8,128)(2,1)} %get-tuple-element.43), channel_id=1, source_target_pairs={{0,4},{2,6},{4,8},{6,10},{1,5},{3,7},{5,9},{7,11},{16,20},{18,22},... | collective-permute-start | bytes 1572872 | tf_op jit(solution)/shard_map/ppermute | solution.py:52
  195.0 16.7 %collective-permute-start.32 = (bf16[512,512]{1,0:T(8,128)(2,1)S(1)}, bf16[512,512]{1,0:T(8,128)(2,1)}, u32[]{:S(2)}, u32[]{:S(2)}) collective-permute-start(bf16[512,512]{1,0:T(8,128)(2,1)S(1)} %get-tuple-element.44), channel_id=1, source_target_pairs={{8,4},{10,6},{12,8},{14,10},{9,5},{11,7},{13,9},{15,11},{24,20},{2... | collective-permute-start | bytes 1572872 | tf_op jit(solution)/shard_map/ppermute | solution.py:52
  201.7 19.9 %collective-permute-start.21 = (bf16[512,512]{1,0:T(8,128)(2,1)}, bf16[512,512]{1,0:T(8,128)(2,1)S(1)}, u32[]{:S(2)}, u32[]{:S(2)}) collective-permute-start(bf16[512,512]{1,0:T(8,128)(2,1)} %get-tuple-element.46), channel_id=1, source_target_pairs={{0,4},{2,6},{4,8},{6,10},{1,5},{3,7},{5,9},{7,11},{16,20},{18,22},... | collective-permute-start | bytes 1572872 | tf_op jit(solution)/shard_map/ppermute | solution.py:52
  205.8 17.1 %collective-permute-start.23 = (bf16[512,512]{1,0:T(8,128)(2,1)S(1)}, bf16[512,512]{1,0:T(8,128)(2,1)}, u32[]{:S(2)}, u32[]{:S(2)}) collective-permute-start(bf16[512,512]{1,0:T(8,128)(2,1)S(1)} %get-tuple-element.45), channel_id=1, source_target_pairs={{8,4},{10,6},{12,8},{14,10},{9,5},{11,7},{13,9},{15,11},{24,20},{2... | collective-permute-start | bytes 1572872 | tf_op jit(solution)/shard_map/ppermute | solution.py:52
  209.7 19.3 %collective-permute-start.38 = (bf16[256,512]{1,0:T(8,128)(2,1)S(1)}, bf16[256,512]{1,0:T(8,128)(2,1)S(1)}, u32[]{:S(2)}, u32[]{:S(2)}) collective-permute-start(bf16[256,512]{1,0:T(8,128)(2,1)S(1)} %copy-done.16), channel_id=1, source_target_pairs={{0,2},{2,0},{4,6},{6,4},{8,10},{10,8},{12,14},{14,12},{1,3},{3,1},... | collective-permute-start | bytes 786440 | tf_op jit(solution)/shard_map/ppermute | solution.py:34
  211.1 19.4 %collective-permute-start.39 = (bf16[256,512]{1,0:T(8,128)(2,1)S(1)}, bf16[256,512]{1,0:T(8,128)(2,1)S(1)}, u32[]{:S(2)}, u32[]{:S(2)}) collective-permute-start(bf16[256,512]{1,0:T(8,128)(2,1)S(1)} %copy-done.18), channel_id=1, source_target_pairs={{0,2},{2,0},{4,6},{6,4},{8,10},{10,8},{12,14},{14,12},{1,3},{3,1},... | collective-permute-start | bytes 786440 | tf_op jit(solution)/shard_map/ppermute | solution.py:34
  213.6 19.1 %collective-permute-start.31 = (bf16[512,512]{1,0:T(8,128)(2,1)S(1)}, bf16[512,512]{1,0:T(8,128)(2,1)S(1)}, u32[]{:S(2)}, u32[]{:S(2)}) collective-permute-start(bf16[512,512]{1,0:T(8,128)(2,1)S(1)} %get-tuple-element.47), channel_id=1, source_target_pairs={{0,4},{2,6},{4,8},{6,10},{8,12},{10,14},{1,5},{3,7},{5,9},{7,11},{... | collective-permute-start | bytes 1572872 | tf_op jit(solution)/shard_map/ppermute | solution.py:52
  221.6 15.0 %collective-permute-start.33 = (bf16[512,512]{1,0:T(8,128)(2,1)S(1)}, bf16[512,512]{1,0:T(8,128)(2,1)S(1)}, u32[]{:S(2)}, u32[]{:S(2)}) collective-permute-start(bf16[512,512]{1,0:T(8,128)(2,1)S(1)} %get-tuple-element.48), channel_id=1, source_target_pairs={{4,0},{6,2},{8,4},{10,6},{12,8},{14,10},{5,1},{7,3},{9,5},{11,7},{... | collective-permute-start | bytes 1572872 | tf_op jit(solution)/shard_map/ppermute | solution.py:52
  224.4 19.6 %collective-permute-start.22 = (bf16[512,512]{1,0:T(8,128)(2,1)S(1)}, bf16[512,512]{1,0:T(8,128)(2,1)S(1)}, u32[]{:S(2)}, u32[]{:S(2)}) collective-permute-start(bf16[512,512]{1,0:T(8,128)(2,1)S(1)} %get-tuple-element.50), channel_id=1, source_target_pairs={{0,4},{2,6},{4,8},{6,10},{8,12},{10,14},{1,5},{3,7},{5,9},{7,11},{... | collective-permute-start | bytes 1572872 | tf_op jit(solution)/shard_map/ppermute | solution.py:52
  229.1 18.8 %collective-permute-start.24 = (bf16[512,512]{1,0:T(8,128)(2,1)S(1)}, bf16[512,512]{1,0:T(8,128)(2,1)S(1)}, u32[]{:S(2)}, u32[]{:S(2)}) collective-permute-start(bf16[512,512]{1,0:T(8,128)(2,1)S(1)} %get-tuple-element.49), channel_id=1, source_target_pairs={{4,0},{6,2},{8,4},{10,6},{12,8},{14,10},{5,1},{7,3},{9,5},{11,7},{... | collective-permute-start | bytes 1572872 | tf_op jit(solution)/shard_map/ppermute | solution.py:52
  238.1 12.5 %collective-permute-start.34 = (bf16[256,512]{1,0:T(8,128)(2,1)S(1)}, bf16[256,512]{1,0:T(8,128)(2,1)S(1)}, u32[]{:S(2)}, u32[]{:S(2)}) collective-permute-start(bf16[256,512]{1,0:T(8,128)(2,1)S(1)} %slice.70), channel_id=1, source_target_pairs={{0,2},{2,0},{4,6},{6,4},{8,10},{10,8},{12,14},{14,12},{1,3},{3,1},... | collective-permute-start | bytes 786440 | tf_op jit(solution)/shard_map/ppermute | solution.py:34
  (28 other events, 223.7 us)
